TPU v7x, 256 devices: a whole 4x4x8 slice. The times are simulated.
256 devices in a mesh: gx: 4 (over x), gy: 8 (over y, core), gz: 8 (over z).
Axes of the slice: x: 4, y: 4, z: 8, core: 2. Of those that a mesh axis runs over, the one named last changes fastest.
Arguments:
- field: bfloat16 [512, 512, 2048], P('gx', 'gy', 'gz'), may hold values from -64 to 64
- sketch: float32 [512, 128], replicated, may hold values from -6 to 6
Outputs:
- factor: float32 [512, 128], replicated
- core: bfloat16 [128, 512, 2048], P(('gx', 'gy'), None, 'gz')
All inputs are finite; a program needn't handle non-finite values.
Results may differ from a plain program's by a relative error of at most 0.012.
Values may be sent and summed in bfloat16 or wider, within the bound.
A program may use at most 128 MiB of HBM per device.

v0:
```python
import jax
import jax.numpy as jnp
from jax import lax
from jax.sharding import PartitionSpec as P

ITERS = 2


def orthonormal(gram, sketch):
    basis = sketch
    for sweep in range(ITERS):
        image = jnp.dot(gram, basis, precision=lax.Precision.HIGHEST)
        inner = jnp.dot(image.T, image, precision=lax.Precision.HIGHEST)
        lower = jnp.linalg.cholesky(inner)
        basis = jax.scipy.linalg.solve_triangular(lower, image.T, lower=True).T
    return basis


def shards(field, sketch):
    rows_local, second_local, width_local = field.shape
    gx_count = lax.axis_size("gx")
    gy_count = lax.axis_size("gy")
    ranks = sketch.shape[1]
    fibres = lax.all_to_all(field, "gx", split_axis=1, concat_axis=0, tiled=True)
    piece_second = fibres.shape[1]
    unfolded = fibres.reshape(fibres.shape[0], -1)
    partial_value = lax.dot_general(
        unfolded, unfolded, (((1,), (1,)), ((), ())), preferred_element_type=jnp.float32
    )
    gram = lax.psum(partial_value, ("gx", "gy", "gz"))
    factor = orthonormal(gram, sketch)
    factor_low = factor.astype(jnp.bfloat16)
    truncated = lax.dot_general(
        factor_low, unfolded, (((0,), (0,)), ((), ())), preferred_element_type=jnp.float32
    )
    truncated = truncated.astype(jnp.bfloat16).reshape(ranks, 1, 1, piece_second, width_local)
    moved = lax.all_to_all(
        lax.all_to_all(truncated, "gx", split_axis=0, concat_axis=2, tiled=True),
        "gy",
        split_axis=0,
        concat_axis=1,
        tiled=True,
    )
    core = moved.reshape(ranks // (gx_count * gy_count), -1, width_local)
    return (factor, core)


def solution(mesh):
    return jax.shard_map(
        shards,
        mesh=mesh,
        in_specs=(P("gx", "gy", "gz"), P()),
        out_specs=(P(), P(("gx", "gy"), None, "gz")),
        check_vma=False,
    )
```

profile of v0, /device:TPU:1, one launch (start us, length us, event | category | flops | bytes accessed | tf_op | source)
XLA Modules:
  0.0 435.1 jit_solution(9733903715790161467)
XLA Ops:
  7.2 4.6 %copy.17 = bf16[128,64,256]{2,0,1:T(8,128)(2,1)S(1)} copy(bf16[128,64,256]{2,1,0:T(8,128)(2,1)} %param.5) | data formatting | bytes 8388608 | tf_op args[0]
  11.8 52.3 %all_to_all.48 = bf16[128,64,256]{2,0,1:T(8,128)(2,1)S(1)} all-to-all(bf16[128,64,256]{2,0,1:T(8,128)(2,1)S(1)} %copy.17), channel_id=1, replica_groups=mesh['gx'=4,'gy'=8,'gz'=8] {'gx'}, dimensions={1} | all-to-all | bytes 8388608 | tf_op jit(solution)/shard_map/all_to_all | solution.py:24
  64.1 2.5 copy.18
  66.6 2.2 copy.25
  68.8 1.9 copy-done.1
  70.7 3.3 fusion.12
  74.1 257.1 %all-reduce.2.cloned.1.call-done = f32[512,512]{1,0:T(8,128)} async-done(((f32[512,512]{1,0:T(8,128)}), f32[512,512]{1,0:T(8,128)}) %all-reduce.2.cloned.1.call-update) | async-done | bytes 1048592 | tf_op jit(solution)/shard_map/psum | solution.py:30
  331.2 2.2 fusion.13
  334.1 11.9 %cholesky.44 = f32[128,128]{1,0:T(8,128)S(1)} custom-call(f32[128,128]{1,0:T(8,128)S(1)} %fusion.9), custom_call_target="Cholesky" | custom-call | tf_op jit(solution)/shard_map/jit(cholesky)/cholesky | solution.py:14
  346.1 0.6 compare_reduce_fusion.1
  346.7 0.7 fusion.4
  347.4 9.8 %custom-call.6 = f32[1,128,128]{1,2,0:T(8,128)S(1)} custom-call(f32[1,128,128]{2,1,0:T(8,128)S(1)} %fusion.4), custom_call_target="InvertDiagBlocksLowerTriangular" | custom-call | tf_op jit(solution)/shard_map/jit(_solve_triangular)/triangular_solve | solution.py:15
  357.6 2.2 fusion.15
  360.5 11.7 %cholesky.55 = f32[128,128]{1,0:T(8,128)S(1)} custom-call(f32[128,128]{1,0:T(8,128)S(1)} %fusion.7), custom_call_target="Cholesky" | custom-call | tf_op jit(solution)/shard_map/jit(cholesky)/cholesky | solution.py:14
  372.3 0.6 compare_reduce_fusion
  372.9 0.7 fusion.5
  373.6 9.8 %custom-call.7 = f32[1,128,128]{1,2,0:T(8,128)S(1)} custom-call(f32[1,128,128]{2,1,0:T(8,128)S(1)} %fusion.5), custom_call_target="InvertDiagBlocksLowerTriangular" | custom-call | tf_op jit(solution)/shard_map/jit(_solve_triangular)/triangular_solve | solution.py:15
  383.8 2.9 convolution_convert_fusion
  387.0 16.2 %all_to_all.49 = bf16[128,1,1,16,256]{4,3,2,1,0:T(8,128)(2,1)S(1)} all-to-all(bf16[128,1,1,16,256]{4,3,2,1,0:T(8,128)(2,1)S(1)} %bitcast.62), channel_id=1, replica_groups=mesh['gx'=4,'gy'=8,'gz'=8] {'gx'}, dimensions={0} | all-to-all | bytes 2097152 | tf_op jit(solution)/shard_map/all_to_all | solution.py:38
  403.2 1.1 copy.22
  404.3 7.7 %all-to-all-start.2 = ((bf16[32,1,4,16,256]{4,3,2,1,0:T(8,128)(2,1)}), bf16[32,1,4,16,256]{4,3,2,1,0:T(8,128)(2,1)S(1)}, u32[]{:S(2)}, u32[]{:S(2)}) async-start(bf16[32,1,4,16,256]{4,3,2,1,0:T(8,128)(2,1)} %copy.22), calls=%async_computation.2 | async-start | bytes 2097152 | tf_op jit(solution)/shard_map/all_to_all | solution.py:37
  412.1 0.8 copy.24
  412.9 14.3 %all-to-all-done.2 = bf16[32,1,4,16,256]{4,3,2,1,0:T(8,128)(2,1)S(1)} async-done(((bf16[32,1,4,16,256]{4,3,2,1,0:T(8,128)(2,1)}), bf16[32,1,4,16,256]{4,3,2,1,0:T(8,128)(2,1)S(1)}, u32[]{:S(2)}, u32[]{:S(2)}) %all-to-all-start.2) | async-done | bytes 1048608 | tf_op jit(solution)/shard_map/all_to_all | solution.py:37
  427.2 1.0 copy.23
  (16 shorter events, 2.6 us)
Async XLA Ops:
  7.2 324.0 %copy-start = (f32[512,128]{1,0:T(8,128)S(1)}, f32[512,128]{1,0:T(8,128)}, u32[]{:S(2)}) copy-start(f32[512,128]{1,0:T(8,128)} %param.6) | copy-start | bytes 786436
  7.2 324.0 %all-reduce.2.cloned.1.call-start = ((), (), s32[]{:S(2)}) async-start(), calls=%async_computation.3 | async-start | bytes 2097152 | tf_op jit(solution)/shard_map/psum | solution.py:30
  68.8 1.9 copy-start.1
  404.3 22.8 %all-to-all-start.2 = ((bf16[32,1,4,16,256]{4,3,2,1,0:T(8,128)(2,1)}), bf16[32,1,4,16,256]{4,3,2,1,0:T(8,128)(2,1)S(1)}, u32[]{:S(2)}, u32[]{:S(2)}) async-start(bf16[32,1,4,16,256]{4,3,2,1,0:T(8,128)(2,1)} %copy.22), calls=%async_computation.2 | async-start | bytes 2097152 | tf_op jit(solution)/shard_map/all_to_all | solution.py:37
Sparse Core Ops, SparseCore 0:
  74.2 256.9 all-reduce.1
where the time goes:
time: 435 us
  waiting for transfers between devices  271 us (62%)
  blocking collectives  68.5 us (16%)
  other arithmetic  45.9 us (11%)
  local copies, waits for them, and re-layouts  14.6 us (3%)
  between operations  14.2 us (3%)
  matrix products  12.7 us (3%)
  starting transfers between devices  7.78 us (2%)
    psum x1, waiting for transfers between devices, shards(): gram = lax.psum(partial_value, ('gx', 'gy', 'gz'))  257 us
    all_to_all x1, blocking collectives, shards(): lax.all_to_all(field, 'gx', split_axis=1, concat_axis=0, tiled=True)  52.3 us
    another operation x6, other arithmetic, orthonormal(): lower = jnp.linalg.cholesky(inner)  25 us
    another operation x4, other arithmetic, orthonormal(): basis = jax.scipy.linalg.solve_triangular(lower, image.T, lower=True).T  20.9 us
    all_to_all x1, blocking collectives, shards(): lax.all_to_all(truncated, 'gx', split_axis=0, concat_axis=2, tiled=True)  16.2 us
    all_to_all x1, waiting for transfers between devices, shards(): lax.all_to_all(lax.all_to_all(truncated, 'gx', split_axis=0, concat_axis=...  14.3 us
    unnamed x8, local copies, waits for them, and re-layouts  9.81 us
  transfers between devices with their start and end apart: 2, of which 2 were waited for; matrix products, arithmetic and copies ran while one was open for 0% of the time, Pallas kernels for 0%

commit v1 on v0

v1 whole, which is shorter than its diff:
```python
import functools

import jax
import jax.numpy as jnp
from jax import lax
from jax.experimental import pallas as pl
from jax.experimental.pallas import tpu as pltpu
from jax.sharding import PartitionSpec as P

ITERS = 2
MESH = pl.DeviceIdType.MESH
GX, GY, GZ = 4, 8, 8
YC = GY // 2
PLANE = GX * YC
SUB = 4


def remote(src, dst, send, recv, dev):
    return pltpu.make_async_remote_copy(
        src_ref=src, dst_ref=dst, send_sem=send, recv_sem=recv,
        device_id=dev, device_id_type=MESH,
    )


def swap16():
    row = lax.broadcasted_iota(jnp.int32, (256, 256), 0)
    col = lax.broadcasted_iota(jnp.int32, (256, 256), 1)
    hit = ((row & 15) * 16 + (row >> 4)) == col
    return jnp.where(hit, 1.0, 0.0).astype(jnp.bfloat16)


def gram_kernel(field, xs, gfin, raw, perm, gp, r1, acc, r2, r3, a_send, a_recv, own_sem,
                c_send, c_recv, p_send, p_recv, z_send, z_recv, g_send, g_recv, f_send, f_recv):
    x, y, z = lax.axis_index("gx"), lax.axis_index("gy"), lax.axis_index("gz")
    core, yc = lax.rem(y, 2), lax.div(y, 2)
    other = (x, y + 1 - 2 * core, z)

    def xdev(d):
        return (lax.rem(x + d, GX), y, z)

    def zdev(d):
        return (x, y, lax.rem(z + d, GZ))

    def pdev(d):
        return (lax.rem(x + d // YC, GX), 2 * lax.rem(yc + d % YC, YC) + core, z)

    def pnum(d):
        return lax.rem(x + d // YC + GX, GX) * YC + lax.rem(yc + d % YC, YC)

    def pfrom(d):
        return lax.rem(x - d // YC + GX, GX) * YC + lax.rem(yc - d % YC + YC, YC)

    barrier = pltpu.get_barrier_semaphore()
    peers = [pdev(d) for d in range(1, PLANE)] + [zdev(d) for d in range(1, GZ)] + [other]
    for dev in peers:
        pl.semaphore_signal(barrier, inc=1, device_id=dev, device_id_type=MESH)

    rows = field.shape[0] // SUB
    pieces = 16
    mine = pltpu.make_async_copy(
        field.at[:, pl.ds(pl.multiple_of(x * pieces, pieces), pieces), :], raw.at[0], own_sem
    )
    mine.start()
    perm[...] = swap16()
    pl.semaphore_wait(barrier, len(peers))

    sends = {}
    for d in (1, 3, 2):
        to = lax.rem(x + d, GX)
        for s in range(SUB):
            sends[d, s] = remote(
                field.at[pl.ds(s * rows, rows), pl.ds(pl.multiple_of(to * pieces, pieces), pieces), :],
                raw.at[GX - d, pl.ds(s * rows, rows)],
                a_send.at[d * SUB + s], a_recv.at[(GX - d) * SUB + s], xdev(d),
            )
            sends[d, s].start()

    def relayout(d, s):
        base = pl.multiple_of(lax.rem(x + d, GX) * 128, 128)

        def group(g, carry):
            i0 = s * rows + g * 16
            block = raw[d, pl.ds(i0, 16)].reshape(256, 256)
            out = jnp.dot(perm[...], block, preferred_element_type=jnp.float32).astype(jnp.bfloat16)
            for j in range(16):
                xs[pl.ds(pl.multiple_of(base + i0, 16), 16), j * 256:(j + 1) * 256] = out[j * 16:(j + 1) * 16]
            return carry

        lax.fori_loop(0, rows // 16, group, 0)

    def block(a, b, pos):
        def part(k, total):
            k0 = pl.multiple_of(k * 1024, 1024)
            u = xs[pl.ds(pl.multiple_of(a * 128, 128), 128), pl.ds(k0, 1024)]
            v = xs[pl.ds(pl.multiple_of(b * 128, 128), 128), pl.ds(k0, 1024)]
            return total + lax.dot_general(u, v, (((1,), (1,)), ((), ())), preferred_element_type=jnp.float32)

        out = lax.fori_loop(0, 4, part, jnp.zeros((128, 128), jnp.float32))
        gp[pl.ds(pl.multiple_of(pos * 128, 128), 128), :] = out

    mine.wait()
    for s in range(SUB):
        relayout(0, s)
    m1, p1, p2 = lax.rem(x + 3, GX), lax.rem(x + 1, GX), lax.rem(x + 2, GX)
    block(x, x, x)
    for d in (1, 3):
        for s in range(SUB):
            sends[GX - d, s].wait_recv()
            relayout(d, s)
    block(p1, p1, p1)
    block(m1, m1, m1)
    block(x, p1, 4 + x)
    block(m1, x, 4 + m1)
    odd = lax.rem(x + 1, 2)
    block(odd, odd + 2, 8 + odd)
    for s in range(SUB):
        sends[2, s].wait_recv()
        relayout(2, s)
    block(p2, p2, p2)
    block(p1, p2, 4 + p1)
    block(p2, m1, 4 + p2)
    even = lax.rem(x, 2)
    block(even, even + 2, 8 + even)

    half = 640
    to_other = remote(gp.at[pl.ds(pl.multiple_of((1 - core) * half, half), half)], r1, c_send, c_recv, other)
    to_other.start()
    to_other.wait_recv()
    acc[...] = gp[pl.ds(pl.multiple_of(core * half, half), half)] + r1[...]

    piece = half // PLANE
    me = pnum(0)
    order = [10, 2, 8, 6, 9, 11, 14, 1, 3, 4, 12, 5, 7, 13, 15]
    plane = {}
    for d in order:
        plane[d] = remote(
            acc.at[pl.ds(pl.multiple_of(pnum(d) * piece, 8), piece)], r2.at[me],
            p_send.at[d], p_recv.at[d], pdev(d),
        )
        plane[d].start()
    r2[me] = acc[pl.ds(pl.multiple_of(me * piece, 8), piece)]
    for d in order:
        remote(r2.at[pfrom(d)], r2.at[pfrom(d)], p_send.at[d], p_recv.at[d], pdev(d)).wait_recv()
    total = r2[0]
    for q in range(1, PLANE):
        total = total + r2[q]
    r3[z] = total

    along = {}
    for d in (4, 3, 5, 2, 6, 1, 7):
        along[d] = remote(r3.at[z], r3.at[z], z_send.at[d], z_recv.at[d], zdev(d))
        along[d].start()
    for d in (1, 7, 2, 6, 3, 5, 4):
        src = lax.rem(z - d + GZ, GZ)
        remote(r3.at[src], r3.at[src], z_send.at[d], z_recv.at[d], zdev(d)).wait_recv()
    total = r3[0]
    for q in range(1, GZ):
        total = total + r3[q]

    def place(q):
        return gfin.at[pl.ds(pl.multiple_of(core * half + q * piece, 8), piece)]

    gfin[pl.ds(pl.multiple_of(core * half + me * piece, 8), piece)] = total
    spread = {}
    for d in order:
        spread[d] = remote(place(me), place(me), g_send.at[d], g_recv.at[d], pdev(d))
        spread[d].start()
    onward = {0: remote(place(me), place(me), f_send.at[0], f_recv.at[0], other)}
    onward[0].start()
    for d in order[::-1]:
        at = place(pfrom(d))
        remote(at, at, g_send.at[d], g_recv.at[d], pdev(d)).wait_recv()
        onward[d] = remote(at, at, f_send.at[d], f_recv.at[d], other)
        onward[d].start()
    for d in range(PLANE):
        there = gfin.at[pl.ds(pl.multiple_of((1 - core) * half + pfrom(d) * piece, 8), piece)]
        remote(there, there, f_send.at[d], f_recv.at[d], other).wait_recv()

    for copies in (sends, plane, along, spread, onward):
        for c in copies.values():
            c.wait_send()
    to_other.wait_send()


def core_kernel(factor_t, xs, out, perm, t, buf, send, recv, own_sem):
    x, y, z = lax.axis_index("gx"), lax.axis_index("gy"), lax.axis_index("gz")

    def dev(dx, dy):
        return (lax.rem(x + dx, GX), lax.rem(y + dy, GY), z)

    offsets = [(dx, dy) for dx in (2, 1, 3, 0) for dy in (4, 5, 3, 2, 6, 7, 1, 0)]
    barrier = pltpu.get_barrier_semaphore()
    for dx, dy in offsets[:-1]:
        pl.semaphore_signal(barrier, inc=1, device_id=dev(dx, dy), device_id_type=MESH)
    perm[...] = swap16()

    def product(j, carry):
        cols = pl.ds(pl.multiple_of(j * 256, 256), 256)
        t[:, cols] = jnp.dot(factor_t[...], xs[:, cols], preferred_element_type=jnp.float32).astype(jnp.bfloat16)
        return carry

    lax.fori_loop(0, 16, product, 0)
    pl.semaphore_wait(barrier, len(offsets) - 1)

    def place(px, py):
        return out.at[:, pl.ds(pl.multiple_of(py * 64 + px * 16, 16), 16), :]

    copies = {}
    for dx in (2, 1, 3, 0):
        to = lax.rem(x + dx, GX)

        def group(g, carry):
            r0 = pl.multiple_of(to * 32 + g * 16, 16)
            block = jnp.concatenate([t[pl.ds(r0, 16), j * 256:(j + 1) * 256] for j in range(16)], axis=0)
            rows = jnp.dot(perm[...], block, preferred_element_type=jnp.float32).astype(jnp.bfloat16)
            buf[pl.ds(r0, 16)] = rows.reshape(16, 16, 256)
            return carry

        lax.fori_loop(0, 2, group, 0)
        for k, dy in enumerate((4, 5, 3, 2, 6, 7, 1, 0)):
            src = buf.at[pl.ds(to * 32 + lax.rem(y + dy, GY) * 4, 4)]
            if dx or dy:
                n = dx * GY + dy
                copies[n] = remote(src, place(x, y), send.at[n], recv.at[n], dev(dx, dy))
                copies[n].start()
            else:
                mine = pltpu.make_async_copy(src, place(x, y), own_sem)
                mine.start()
    for dx, dy in offsets[:-1]:
        n = dx * GY + dy
        at = place(lax.rem(x - dx + GX, GX), lax.rem(y - dy + GY, GY))
        remote(at, at, send.at[n], recv.at[n], dev(dx, dy)).wait_recv()
    for c in copies.values():
        c.wait_send()
    mine.wait()


def orthonormal(gram, sketch):
    basis = sketch
    for sweep in range(ITERS):
        image = jnp.dot(gram, basis, precision=lax.Precision.HIGHEST)
        inner = jnp.dot(image.T, image, precision=lax.Precision.HIGHEST)
        lower = jnp.linalg.cholesky(inner)
        basis = jax.scipy.linalg.solve_triangular(lower, image.T, lower=True).T
    return basis


def assemble(packed):
    b = packed.reshape(10, 128, 128)
    grid = [[None] * 4 for _ in range(4)]
    for a in range(4):
        grid[a][a] = b[a]
        n = (a + 1) % 4
        grid[a][n], grid[n][a] = b[4 + a], b[4 + a].T
    for a in range(2):
        grid[a][a + 2], grid[a + 2][a] = b[8 + a], b[8 + a].T
    return jnp.block(grid)


VMEM = pl.BlockSpec(memory_space=pltpu.VMEM)
ANY = pl.BlockSpec(memory_space=pl.ANY)
DMA = pltpu.SemaphoreType.DMA


def shards(field, sketch):
    xs, packed = pl.pallas_call(
        gram_kernel,
        out_shape=(
            jax.ShapeDtypeStruct((512, 4096), jnp.bfloat16),
            jax.ShapeDtypeStruct((1280, 128), jnp.float32),
        ),
        in_specs=[ANY],
        out_specs=(VMEM, VMEM),
        scratch_shapes=[
            pltpu.VMEM((GX, 128, 16, 256), jnp.bfloat16),
            pltpu.VMEM((256, 256), jnp.bfloat16),
            pltpu.VMEM((1280, 128), jnp.float32),
            pltpu.VMEM((640, 128), jnp.float32),
            pltpu.VMEM((640, 128), jnp.float32),
            pltpu.VMEM((PLANE, 40, 128), jnp.float32),
            pltpu.VMEM((GZ, 40, 128), jnp.float32),
            DMA((GX * SUB,)), DMA((GX * SUB,)), DMA,
            DMA, DMA,
            DMA((PLANE,)), DMA((PLANE,)),
            DMA((GZ,)), DMA((GZ,)),
            DMA((PLANE,)), DMA((PLANE,)),
            DMA((PLANE,)), DMA((PLANE,)),
        ],
        compiler_params=pltpu.CompilerParams(
            collective_id=0, has_side_effects=True, vmem_limit_bytes=40 * 2**20
        ),
        name="gram",
    )(field)
    factor = orthonormal(assemble(packed), sketch)
    factor_t = factor.astype(jnp.bfloat16).T
    core = pl.pallas_call(
        core_kernel,
        out_shape=jax.ShapeDtypeStruct((4, 512, 256), jnp.bfloat16),
        in_specs=[VMEM, VMEM],
        out_specs=ANY,
        scratch_shapes=[
            pltpu.VMEM((256, 256), jnp.bfloat16),
            pltpu.VMEM((128, 4096), jnp.bfloat16),
            pltpu.VMEM((128, 16, 256), jnp.bfloat16),
            DMA((GX * GY,)), DMA((GX * GY,)), DMA,
        ],
        compiler_params=pltpu.CompilerParams(
            collective_id=1, has_side_effects=True, vmem_limit_bytes=40 * 2**20
        ),
        name="core",
    )(factor_t, xs)
    return (factor, core)


def solution(mesh):
    return jax.shard_map(
        shards,
        mesh=mesh,
        in_specs=(P("gx", "gy", "gz"), P()),
        out_specs=(P(), P(("gx", "gy"), None, "gz")),
        check_vma=False,
    )
```

time: 435 us -> 164 us (0.38)
  waiting for transfers between devices: 271 us -> 0 us
  Pallas kernels: 0 us -> 104 us
  blocking collectives: 68.5 us -> 0 us
  between operations: 14.2 us -> 0.86 us
  matrix products: 12.7 us -> 3.97 us
  starting transfers between devices: 7.78 us -> 0 us
  local copies, waits for them, and re-layouts: 14.6 us -> 9.02 us
    psum x1 -> x0, waiting for transfers between devices: 257 us -> none  [shards(): gram = lax.psum(partial_value, ('gx', 'gy', 'gz'))]
    pallas_call x0 -> x2, Pallas kernels: none -> 104 us  [the longest x1 84.8 us: shards(): pl.pallas_call(gram_kernel, out_shape=(jax.ShapeDtypeStruct((512, 4096),...]
    all_to_all x2 -> x0, blocking collectives: 68.5 us -> none  [the longest x1 52.3 us: shards(): lax.all_to_all(field, 'gx', split_axis=1, concat_axis=0, tiled=True)]
    all_to_all x1 -> x0, waiting for transfers between devices: 14.3 us -> none  [shards(): lax.all_to_all(lax.all_to_all(truncated, 'gx', split_axis=0, concat_axis=...]
    all_to_all x1 -> x0, starting transfers between devices: 7.74 us -> none  [shards(): lax.all_to_all(lax.all_to_all(truncated, 'gx', split_axis=0, concat_axis=...]
    dot_general x2 -> x0, matrix products: 6.24 us -> none  [the longest x1 3.33 us: shards(): lax.dot_general(unfolded, unfolded, (((1,), (1,)), ((), ())), preferred_e...]
    all_to_all x3 -> x0, local copies, waits for them, and re-layouts: 4.61 us -> none  [the longest x1 2.46 us: shards(): lax.all_to_all(field, 'gx', split_axis=1, concat_axis=0, tiled=True)]
    unnamed x8 -> x10, local copies, waits for them, and re-layouts: 9.81 us -> 8.14 us
  transfers between devices with their start and end apart: 2 -> 0, of which waited for: 2 -> 0; matrix products, arithmetic and copies ran while one was open for 0% -> 0% of each run, Pallas kernels for 0% -> 0%
where the time goes in v1:
time: 164 us; the launch traced here: 163 us
  Pallas kernels  104 us (63%)
  other arithmetic  46 us (28%)
  local copies, waits for them, and re-layouts  9.02 us (6%)
  matrix products  3.97 us (2%)
    pallas_call x1, Pallas kernels, shards(): pl.pallas_call(gram_kernel, out_shape=(jax.ShapeDtypeStruct((512, 4096),...  84.8 us
    another operation x6, other arithmetic, orthonormal(): lower = jnp.linalg.cholesky(inner)  25 us
    another operation x4, other arithmetic, orthonormal(): basis = jax.scipy.linalg.solve_triangular(lower, image.T, lower=True).T  20.9 us
    pallas_call x1, Pallas kernels, shards(): pl.pallas_call(core_kernel, out_shape=jax.ShapeDtypeStruct((4, 512, 256),...  18.8 us
    unnamed x10, local copies, waits for them, and re-layouts  8.14 us

profile of v1, /device:TPU:1, one launch (start us, length us, event | category | flops | bytes accessed | tf_op | source)
XLA Modules:
  0.0 163.4 jit_solution(17659756586642302842)
XLA Ops:
  0.7 2.2 %copy-done.1 = bf16[128,64,256]{2,1,0:T(8,128)(2,1)S(1)} copy-done((bf16[128,64,256]{2,1,0:T(8,128)(2,1)S(1)}, bf16[128,64,256]{2,1,0:T(8,128)(2,1)}, u32[]{:S(2)}) %copy-start.1) | copy-done | bytes 4194328
  2.9 84.8 %gram.1 = (bf16[512,4096]{1,0:T(8,128)(2,1)S(1)}, f32[1280,128]{1,0:T(8,128)S(1)}) custom-call(bf16[128,64,256]{2,1,0:T(8,128)(2,1)S(1)} %copy-done.1), custom_call_target="tpu_custom_call" | custom-call | tf_op jit(solution)/shard_map/gram/pallas_call | solution.py:266
  87.6 1.9 %copy-done.2 = bf16[512,4096]{1,0:T(8,128)(2,1)} copy-done((bf16[512,4096]{1,0:T(8,128)(2,1)}, bf16[512,4096]{1,0:T(8,128)(2,1)S(1)}, u32[]{:S(2)}) %copy-start.2) | copy-done | bytes 4194328
  89.6 0.2 copy.4
  89.9 0.1 copy.11
  90.2 0.1 copy.10
  90.5 1.0 fusion.14
  91.4 0.6 fusion.15
  92.2 11.7 %cholesky.44 = f32[128,128]{1,0:T(8,128)S(1)} custom-call(f32[128,128]{1,0:T(8,128)S(1)} %fusion.9), custom_call_target="Cholesky" | custom-call | tf_op jit(solution)/shard_map/jit(cholesky)/cholesky | solution.py:243
  103.9 0.6 compare_reduce_fusion.1
  104.5 0.7 fusion.4
  105.2 9.8 %custom-call.6 = f32[1,128,128]{1,2,0:T(8,128)S(1)} custom-call(f32[1,128,128]{2,1,0:T(8,128)S(1)} %fusion.4), custom_call_target="InvertDiagBlocksLowerTriangular" | custom-call | tf_op jit(solution)/shard_map/jit(_solve_triangular)/triangular_solve | solution.py:244
  115.0 0.4 fusion.2
  115.4 1.0 fusion.16
  116.4 0.6 fusion.17
  117.1 11.9 %cholesky.55 = f32[128,128]{1,0:T(8,128)S(1)} custom-call(f32[128,128]{1,0:T(8,128)S(1)} %fusion.7), custom_call_target="Cholesky" | custom-call | tf_op jit(solution)/shard_map/jit(cholesky)/cholesky | solution.py:243
  129.1 0.6 compare_reduce_fusion
  129.7 0.7 fusion.5
  130.4 9.8 %custom-call.7 = f32[1,128,128]{1,2,0:T(8,128)S(1)} custom-call(f32[1,128,128]{2,1,0:T(8,128)S(1)} %fusion.5), custom_call_target="InvertDiagBlocksLowerTriangular" | custom-call | tf_op jit(solution)/shard_map/jit(_solve_triangular)/triangular_solve | solution.py:244
  140.2 0.4 fusion.13
  140.6 2.2 %copy-done.3 = bf16[512,4096]{1,0:T(8,128)(2,1)S(1)} copy-done((bf16[512,4096]{1,0:T(8,128)(2,1)S(1)}, bf16[512,4096]{1,0:T(8,128)(2,1)}, u32[]{:S(2)}) %copy-start.3) | copy-done | bytes 4194328
  142.8 18.8 %core.1 = bf16[4,512,256]{2,1,0:T(8,128)(2,1)S(1)} custom-call(bf16[128,512]{1,0:T(8,128)(2,1)S(1)} %get-tuple-element.26.factor_t, bf16[512,4096]{1,0:T(8,128)(2,1)S(1)} %copy-done.3), custom_call_target="tpu_custom_call" | custom-call | tf_op jit(solution)/shard_map/core/pallas_call | solution.py:296
  161.6 0.8 copy.14
  162.5 1.0 copy.16
  (17 shorter events, 0.6 us)
Async XLA Ops:
  0.6 89.8 %copy-start = (f32[512,128]{1,0:T(8,128)S(1)}, f32[512,128]{1,0:T(8,128)}, u32[]{:S(2)}) copy-start(f32[512,128]{1,0:T(8,128)} %param.6) | copy-start | bytes 786436
  0.6 2.2 %copy-start.1 = (bf16[128,64,256]{2,1,0:T(8,128)(2,1)S(1)}, bf16[128,64,256]{2,1,0:T(8,128)(2,1)}, u32[]{:S(2)}) copy-start(bf16[128,64,256]{2,1,0:T(8,128)(2,1)} %field.1) | copy-start | bytes 12582916
  87.6 1.9 %copy-start.2 = (bf16[512,4096]{1,0:T(8,128)(2,1)}, bf16[512,4096]{1,0:T(8,128)(2,1)S(1)}, u32[]{:S(2)}) copy-start(bf16[512,4096]{1,0:T(8,128)(2,1)S(1)} %get-tuple-element.7.xs) | copy-start | bytes 12582916
  140.6 2.2 %copy-start.3 = (bf16[512,4096]{1,0:T(8,128)(2,1)S(1)}, bf16[512,4096]{1,0:T(8,128)(2,1)}, u32[]{:S(2)}) copy-start(bf16[512,4096]{1,0:T(8,128)(2,1)} %copy-done.2) | copy-start | bytes 12582916

commit v2 on v1

--- a/solution.py
+++ b/solution.py
@@ -29,7 +29,7 @@
     return jnp.where(hit, 1.0, 0.0).astype(jnp.bfloat16)
 
 
-def gram_kernel(field, xs, gfin, raw, perm, gp, r1, acc, r2, r3, a_send, a_recv, own_sem,
+def gram_kernel(field, xs_out, gfin, raw, xs, out_sem, perm, gp, r1, acc, r2, r3, a_send, a_recv, own_sem,
                 c_send, c_recv, p_send, p_recv, z_send, z_recv, g_send, g_recv, f_send, f_recv):
     x, y, z = lax.axis_index("gx"), lax.axis_index("gy"), lax.axis_index("gz")
     core, yc = lax.rem(y, 2), lax.div(y, 2)
@@ -88,6 +88,12 @@
 
         lax.fori_loop(0, rows // 16, group, 0)
 
+    def keep(d):
+        rows_of = pl.ds(pl.multiple_of(lax.rem(x + d, GX) * 128, 128), 128)
+        out = pltpu.make_async_copy(xs.at[rows_of], xs_out.at[rows_of], out_sem.at[d])
+        out.start()
+        return out
+
     def block(a, b, pos):
         def part(k, total):
             k0 = pl.multiple_of(k * 1024, 1024)
@@ -101,12 +107,14 @@
     mine.wait()
     for s in range(SUB):
         relayout(0, s)
+    kept = [keep(0)]
     m1, p1, p2 = lax.rem(x + 3, GX), lax.rem(x + 1, GX), lax.rem(x + 2, GX)
     block(x, x, x)
     for d in (1, 3):
         for s in range(SUB):
             sends[GX - d, s].wait_recv()
             relayout(d, s)
+        kept.append(keep(d))
     block(p1, p1, p1)
     block(m1, m1, m1)
     block(x, p1, 4 + x)
@@ -116,6 +124,7 @@
     for s in range(SUB):
         sends[2, s].wait_recv()
         relayout(2, s)
+    kept.append(keep(2))
     block(p2, p2, p2)
     block(p1, p2, 4 + p1)
     block(p2, m1, 4 + p2)
@@ -180,9 +189,11 @@
         for c in copies.values():
             c.wait_send()
     to_other.wait_send()
-
-
-def core_kernel(factor_t, xs, out, perm, t, buf, send, recv, own_sem):
+    for c in kept:
+        c.wait()
+
+
+def core_kernel(factor_t, xs_in, out, xs, in_sem, perm, t, buf, send, recv, own_sem):
     x, y, z = lax.axis_index("gx"), lax.axis_index("gy"), lax.axis_index("gz")
 
     def dev(dx, dy):
@@ -192,6 +203,11 @@
     barrier = pltpu.get_barrier_semaphore()
     for dx, dy in offsets[:-1]:
         pl.semaphore_signal(barrier, inc=1, device_id=dev(dx, dy), device_id_type=MESH)
+    loads = []
+    for k in range(4):
+        cols = slice(k * 1024, (k + 1) * 1024)
+        loads.append(pltpu.make_async_copy(xs_in.at[:, cols], xs.at[:, cols], in_sem.at[k]))
+        loads[k].start()
     perm[...] = swap16()
 
     def product(j, carry):
@@ -199,7 +215,9 @@
         t[:, cols] = jnp.dot(factor_t[...], xs[:, cols], preferred_element_type=jnp.float32).astype(jnp.bfloat16)
         return carry
 
-    lax.fori_loop(0, 16, product, 0)
+    for k in range(4):
+        loads[k].wait()
+        lax.fori_loop(4 * k, 4 * k + 4, product, 0)
     pl.semaphore_wait(barrier, len(offsets) - 1)
 
     def place(px, py):
@@ -235,26 +253,84 @@
     mine.wait()
 
 
-def orthonormal(gram, sketch):
-    basis = sketch
-    for sweep in range(ITERS):
-        image = jnp.dot(gram, basis, precision=lax.Precision.HIGHEST)
-        inner = jnp.dot(image.T, image, precision=lax.Precision.HIGHEST)
-        lower = jnp.linalg.cholesky(inner)
-        basis = jax.scipy.linalg.solve_triangular(lower, image.T, lower=True).T
-    return basis
-
-
-def assemble(packed):
-    b = packed.reshape(10, 128, 128)
-    grid = [[None] * 4 for _ in range(4)]
-    for a in range(4):
-        grid[a][a] = b[a]
-        n = (a + 1) % 4
-        grid[a][n], grid[n][a] = b[4 + a], b[4 + a].T
-    for a in range(2):
-        grid[a][a + 2], grid[a + 2][a] = b[8 + a], b[8 + a].T
-    return jnp.block(grid)
+def split3(q):
+    a = q.astype(jnp.bfloat16).astype(jnp.float32)
+    b = (q - a).astype(jnp.bfloat16).astype(jnp.float32)
+    return a, b, q - a - b
+
+
+def eliminate(a, d, base):
+    lane = lax.broadcasted_iota(jnp.int32, (8, 128), 1)
+    sub = lax.broadcasted_iota(jnp.int32, (8, 128), 0)
+    inside = (lane >= base) & (lane < base + 8)
+    rows = [jnp.broadcast_to(a[base + i:base + i + 1, :], (8, 128)) for i in range(8)]
+    s = [[jnp.broadcast_to(rows[i][:, base + k:base + k + 1], (8, 128)) for k in range(i + 1)] for i in range(8)]
+    w = [jnp.where(inside, jnp.where(lane == base + i, 1.0, 0.0), rows[i]) for i in range(8)]
+    inverse = []
+    for k in range(8):
+        inverse.append(1.0 / s[k][k])
+        for i in range(k + 1, 8):
+            m = s[i][k] * inverse[k]
+            for l in range(k + 1, i + 1):
+                s[i][l] = s[i][l] - m * s[l][k]
+            w[i] = w[i] - m * w[k]
+    p, scale, pivot = w[0], inverse[0], s[0][0]
+    for i in range(1, 8):
+        p = jnp.where(sub == i, w[i], p)
+        scale = jnp.where(sub == i, inverse[i], scale)
+        pivot = jnp.where(sub == i, s[i][i], pivot)
+    d[base:base + 8, :] = pivot
+    return p, p * scale, inside
+
+
+def inverse_cholesky(a, d):
+    for base in range(0, 128, 8):
+        p, scaled, inside = eliminate(a, d, base)
+        a[base:base + 8, :] = p
+        after = base + 8
+        if after < 128:
+            u, v = split3(p), split3(scaled)
+            left = jnp.concatenate([u[0], u[0], u[1], u[0], u[1], u[2]], axis=0)
+            right = jnp.concatenate([v[0], v[1], v[0], v[2], v[1], v[0]], axis=0).astype(jnp.bfloat16)
+            change = jnp.dot(left.T.astype(jnp.bfloat16), right, preferred_element_type=jnp.float32)
+            old = a[after:, :]
+            a[after:, :] = jnp.where(jnp.broadcast_to(inside[:1], old.shape), 0.0, old) - change[after:, :]
+
+
+def exact_dot(u, v, dims=((1,), (0,))):
+    return lax.dot_general(u, v, (dims, ((), ())), precision=lax.Precision.HIGHEST, preferred_element_type=jnp.float32)
+
+
+def factor_kernel(packed, sketch, factor, factor_t, gram, basis, image, a, d):
+    def block(k):
+        return packed[128 * k:128 * k + 128, :]
+
+    def put(i, j, value):
+        gram[128 * i:128 * i + 128, 128 * j:128 * j + 128] = value
+
+    for k in range(4):
+        put(k, k, block(k))
+        n = (k + 1) % 4
+        put(k, n, block(4 + k))
+        put(n, k, block(4 + k).T)
+    for k in range(2):
+        put(k, k + 2, block(8 + k))
+        put(k + 2, k, block(8 + k).T)
+    basis[...] = sketch[...].T
+
+    def sweep(step, carry):
+        image[...] = exact_dot(basis[...], gram[...])
+        a[...] = exact_dot(image[...], image[...], ((1,), (1,)))
+        inverse_cholesky(a, d)
+        row = lax.broadcasted_iota(jnp.int32, (128, 128), 0)
+        col = lax.broadcasted_iota(jnp.int32, (128, 128), 1)
+        lower = jnp.where(col <= row, a[...] * lax.rsqrt(d[...]), 0.0)
+        basis[...] = exact_dot(lower, image[...])
+        return carry
+
+    lax.fori_loop(0, ITERS, sweep, 0)
+    factor_t[...] = basis[...].astype(jnp.bfloat16)
+    factor[...] = basis[...].T
 
 
 VMEM = pl.BlockSpec(memory_space=pltpu.VMEM)
@@ -270,9 +346,11 @@
             jax.ShapeDtypeStruct((1280, 128), jnp.float32),
         ),
         in_specs=[ANY],
-        out_specs=(VMEM, VMEM),
+        out_specs=(ANY, VMEM),
         scratch_shapes=[
             pltpu.VMEM((GX, 128, 16, 256), jnp.bfloat16),
+            pltpu.VMEM((512, 4096), jnp.bfloat16),
+            DMA((GX,)),
             pltpu.VMEM((256, 256), jnp.bfloat16),
             pltpu.VMEM((1280, 128), jnp.float32),
             pltpu.VMEM((640, 128), jnp.float32),
@@ -287,25 +365,43 @@
             DMA((PLANE,)), DMA((PLANE,)),
         ],
         compiler_params=pltpu.CompilerParams(
-            collective_id=0, has_side_effects=True, vmem_limit_bytes=40 * 2**20
+            collective_id=0, has_side_effects=True, vmem_limit_bytes=60 * 2**20
         ),
         name="gram",
     )(field)
-    factor = orthonormal(assemble(packed), sketch)
-    factor_t = factor.astype(jnp.bfloat16).T
+    factor, factor_t = pl.pallas_call(
+        factor_kernel,
+        out_shape=(
+            jax.ShapeDtypeStruct((512, 128), jnp.float32),
+            jax.ShapeDtypeStruct((128, 512), jnp.bfloat16),
+        ),
+        in_specs=[VMEM, VMEM],
+        out_specs=(VMEM, VMEM),
+        scratch_shapes=[
+            pltpu.VMEM((512, 512), jnp.float32),
+            pltpu.VMEM((128, 512), jnp.float32),
+            pltpu.VMEM((128, 512), jnp.float32),
+            pltpu.VMEM((128, 128), jnp.float32),
+            pltpu.VMEM((128, 128), jnp.float32),
+        ],
+        compiler_params=pltpu.CompilerParams(vmem_limit_bytes=60 * 2**20),
+        name="factor",
+    )(packed, sketch)
     core = pl.pallas_call(
         core_kernel,
         out_shape=jax.ShapeDtypeStruct((4, 512, 256), jnp.bfloat16),
-        in_specs=[VMEM, VMEM],
+        in_specs=[VMEM, ANY],
         out_specs=ANY,
         scratch_shapes=[
+            pltpu.VMEM((512, 4096), jnp.bfloat16),
+            DMA((4,)),
             pltpu.VMEM((256, 256), jnp.bfloat16),
             pltpu.VMEM((128, 4096), jnp.bfloat16),
             pltpu.VMEM((128, 16, 256), jnp.bfloat16),
             DMA((GX * GY,)), DMA((GX * GY,)), DMA,
         ],
         compiler_params=pltpu.CompilerParams(
-            collective_id=1, has_side_effects=True, vmem_limit_bytes=40 * 2**20
+            collective_id=1, has_side_effects=True, vmem_limit_bytes=60 * 2**20
         ),
         name="core",
     )(factor_t, xs)

time: 164 us -> 127 us (0.77)
  other arithmetic: 46 us -> 0 us
  Pallas kernels: 104 us -> 124 us
  local copies, waits for them, and re-layouts: 9.02 us -> 2.26 us
  matrix products: 3.97 us -> 0 us
    another operation x10 -> x0, other arithmetic: 45.9 us -> none  [the longest x6 25 us: orthonormal(): lower = jnp.linalg.cholesky(inner)]
    pallas_call x0 -> x1, Pallas kernels: none -> 17.5 us  [shards(): pl.pallas_call(factor_kernel, out_shape=(jax.ShapeDtypeStruct((512, 128),...]
    unnamed x10 -> x1, local copies, waits for them, and re-layouts: 8.14 us -> 2.26 us
    dot_general x4 -> x0, matrix products: 3.14 us -> none  [the longest x2 1.96 us: orthonormal(): image = jnp.dot(gram, basis, precision=lax.Precision.HIGHEST)]
    pallas_call x1, Pallas kernels: 18.8 us -> 20.9 us  [shards(): pl.pallas_call(core_kernel, out_shape=jax.ShapeDtypeStruct((4, 512, 256),...]
where the time goes in v2:
time: 127 us
  Pallas kernels  124 us (98%)
  local copies, waits for them, and re-layouts  2.26 us (2%)
    pallas_call x1, Pallas kernels, shards(): pl.pallas_call(gram_kernel, out_shape=(jax.ShapeDtypeStruct((512, 4096),...  86 us
    pallas_call x1, Pallas kernels, shards(): pl.pallas_call(core_kernel, out_shape=jax.ShapeDtypeStruct((4, 512, 256),...  20.9 us
    pallas_call x1, Pallas kernels, shards(): pl.pallas_call(factor_kernel, out_shape=(jax.ShapeDtypeStruct((512, 128),...  17.5 us

profile of v2, /device:TPU:1, one launch (start us, length us, event | category | flops | bytes accessed | tf_op | source)
XLA Modules:
  0.0 127.3 jit_solution(2427170854841002009)
XLA Ops:
  0.6 86.0 %gram.1 = (bf16[512,4096]{1,0:T(8,128)(2,1)}, f32[1280,128]{1,0:T(8,128)}) custom-call(bf16[128,64,256]{2,1,0:T(8,128)(2,1)} %field.1), custom_call_target="tpu_custom_call" | custom-call | tf_op jit(solution)/shard_map/gram/pallas_call | solution.py:342
  86.6 17.5 %factor.1 = (f32[512,128]{1,0:T(8,128)}, bf16[128,512]{1,0:T(8,128)(2,1)}) custom-call(f32[1280,128]{1,0:T(8,128)} %get-tuple-element.6.packed, f32[512,128]{1,0:T(8,128)} %sketch.1), custom_call_target="tpu_custom_call" | custom-call | tf_op jit(solution)/shard_map/factor/pallas_call | solution.py:372
  104.1 20.9 %core.1 = bf16[4,512,256]{2,1,0:T(8,128)(2,1)} custom-call(bf16[128,512]{1,0:T(8,128)(2,1)} %get-tuple-element.8.factor_t, bf16[512,4096]{1,0:T(8,128)(2,1)} %get-tuple-element.9.xs_in), custom_call_target="tpu_custom_call" | custom-call | tf_op jit(solution)/shard_map/core/pallas_call | solution.py:390
  125.0 2.3 %copy.5 = bf16[4,512,256]{2,1,0:T(8,128)(2,1)} copy(bf16[4,512,256]{2,1,0:T(8,128)(2,1)} %core.1) | data formatting | bytes 2097152

commit v3 on v1

--- a/solution.py
+++ b/solution.py
@@ -235,26 +235,116 @@
     mine.wait()
 
 
-def orthonormal(gram, sketch):
-    basis = sketch
-    for sweep in range(ITERS):
-        image = jnp.dot(gram, basis, precision=lax.Precision.HIGHEST)
-        inner = jnp.dot(image.T, image, precision=lax.Precision.HIGHEST)
-        lower = jnp.linalg.cholesky(inner)
-        basis = jax.scipy.linalg.solve_triangular(lower, image.T, lower=True).T
-    return basis
-
-
-def assemble(packed):
-    b = packed.reshape(10, 128, 128)
-    grid = [[None] * 4 for _ in range(4)]
-    for a in range(4):
-        grid[a][a] = b[a]
-        n = (a + 1) % 4
-        grid[a][n], grid[n][a] = b[4 + a], b[4 + a].T
-    for a in range(2):
-        grid[a][a + 2], grid[a + 2][a] = b[8 + a], b[8 + a].T
-    return jnp.block(grid)
+def split3(q):
+    a = q.astype(jnp.bfloat16).astype(jnp.float32)
+    b = (q - a).astype(jnp.bfloat16).astype(jnp.float32)
+    return a, b, q - a - b
+
+
+def total_of(terms):
+    while len(terms) > 1:
+        terms = [terms[i] + terms[i + 1] if i + 1 < len(terms) else terms[i] for i in range(0, len(terms), 2)]
+    return terms[0]
+
+
+def inverse_cholesky(a, d):
+    lane = lax.broadcasted_iota(jnp.int32, (8, 128), 1)
+    sub = lax.broadcasted_iota(jnp.int32, (8, 128), 0)
+
+    def repeat(v, l):
+        return jnp.broadcast_to(v[:, l:l + 1], (8, 128))
+
+    rows = [jnp.broadcast_to(a[i:i + 1, :], (8, 128)) for i in range(8)]
+    for base in range(0, 128, 8):
+        inside = (lane >= base) & (lane < base + 8)
+        s = [[repeat(rows[i], base + k) for k in range(i + 1)] for i in range(8)]
+        w = [jnp.where(inside, jnp.where(lane == base + i, 1.0, 0.0), rows[i]) for i in range(8)]
+        inverse = []
+        for k in range(8):
+            inverse.append(1.0 / s[k][k])
+            for i in range(k + 1, 8):
+                m = s[i][k] * inverse[k]
+                for l in range(k + 1, i + 1):
+                    s[i][l] = s[i][l] - m * s[l][k]
+                w[i] = w[i] - m * w[k]
+        p, scale, pivot = w[0], inverse[0], s[0][0]
+        for i in range(1, 8):
+            p = jnp.where(sub == i, w[i], p)
+            scale = jnp.where(sub == i, inverse[i], scale)
+            pivot = jnp.where(sub == i, s[i][i], pivot)
+        a[base:base + 8, :] = p
+        d[base:base + 8, :] = pivot
+        now, after = base + 8, base + 16
+        if now < 128:
+            before = [jnp.broadcast_to(a[now + i:now + i + 1, :], (8, 128)) for i in range(8)]
+            rows = [
+                jnp.where(inside, 0.0, before[i])
+                - total_of([repeat(w[k], now + i) * inverse[k] * w[k] for k in range(8)])
+                for i in range(8)
+            ]
+        if after < 128:
+            u, v = split3(p), split3(p * scale)
+            left = jnp.concatenate([u[0], u[0], u[1], u[0], u[1], u[2]], axis=0).astype(jnp.bfloat16)
+            right = jnp.concatenate([v[0], v[1], v[0], v[2], v[1], v[0]], axis=0).astype(jnp.bfloat16)
+            change = lax.dot_general(left, right, (((0,), (0,)), ((), ())), preferred_element_type=jnp.float32)
+            old = a[after:, :]
+            a[after:, :] = jnp.where(jnp.broadcast_to(inside[:1], old.shape), 0.0, old) - change[after:, :]
+
+
+def exact_dot(u, v, dims=((1,), (0,))):
+    return lax.dot_general(u, v, (dims, ((), ())), precision=lax.Precision.HIGHEST, preferred_element_type=jnp.float32)
+
+
+def factor_kernel(packed, sketch, factor, factor_t, gram, basis, image, a, d, diagonal):
+    def block(k):
+        return packed[128 * k:128 * k + 128, :]
+
+    def put(i, j, value):
+        gram[128 * i:128 * i + 128, 128 * j:128 * j + 128] = value
+
+    for k in range(4):
+        put(k, k, block(k))
+        n = (k + 1) % 4
+        put(k, n, block(4 + k))
+        put(n, k, block(4 + k).T)
+    for k in range(2):
+        put(k, k + 2, block(8 + k))
+        put(k + 2, k, block(8 + k).T)
+    start = sketch[...].T
+    row = lax.broadcasted_iota(jnp.int32, (128, 128), 0)
+    col = lax.broadcasted_iota(jnp.int32, (128, 128), 1)
+
+    def orthonormalize():
+        inner = exact_dot(image[...], image[...], ((1,), (1,)))
+        a[...] = inner
+        diagonal[...] = jnp.where(row == col, inner, 0.0)
+        inverse_cholesky(a, d)
+        lower = jnp.where(col <= row, a[...] * lax.rsqrt(d[...]), 0.0)
+        basis[...] = exact_dot(lower, image[...])
+
+    def finish():
+        factor_t[...] = basis[...].astype(jnp.bfloat16)
+        factor[...] = basis[...].T
+
+    first = exact_dot(start, gram[...])
+    first = first * lax.rsqrt(jnp.sum(first * first, axis=1, keepdims=True))
+    image[...] = exact_dot(first, gram[...])
+    orthonormalize()
+    finish()
+    kept = jnp.where(row == col, d[...], 1.0) >= 1e-3 * diagonal[...]
+    small = jnp.sum(jnp.where(kept, 0.0, 1.0))
+
+    @pl.when(small > 0.0)
+    def _():
+        basis[...] = start
+
+        def sweep(step, carry):
+            image[...] = exact_dot(basis[...], gram[...])
+            orthonormalize()
+            return carry
+
+        lax.fori_loop(0, ITERS, sweep, 0)
+        finish()
 
 
 VMEM = pl.BlockSpec(memory_space=pltpu.VMEM)
@@ -269,7 +359,7 @@
             jax.ShapeDtypeStruct((512, 4096), jnp.bfloat16),
             jax.ShapeDtypeStruct((1280, 128), jnp.float32),
         ),
-        in_specs=[ANY],
+        in_specs=[pl.BlockSpec(memory_space=pltpu.HBM)],
         out_specs=(VMEM, VMEM),
         scratch_shapes=[
             pltpu.VMEM((GX, 128, 16, 256), jnp.bfloat16),
@@ -287,17 +377,34 @@
             DMA((PLANE,)), DMA((PLANE,)),
         ],
         compiler_params=pltpu.CompilerParams(
-            collective_id=0, has_side_effects=True, vmem_limit_bytes=40 * 2**20
+            collective_id=0, has_side_effects=True, vmem_limit_bytes=24 * 2**20
         ),
         name="gram",
-    )(field)
-    factor = orthonormal(assemble(packed), sketch)
-    factor_t = factor.astype(jnp.bfloat16).T
+    )(pltpu.with_memory_space_constraint(field, pltpu.HBM))
+    factor, factor_t = pl.pallas_call(
+        factor_kernel,
+        out_shape=(
+            jax.ShapeDtypeStruct((512, 128), jnp.float32),
+            jax.ShapeDtypeStruct((128, 512), jnp.bfloat16),
+        ),
+        in_specs=[VMEM, VMEM],
+        out_specs=(VMEM, VMEM),
+        scratch_shapes=[
+            pltpu.VMEM((512, 512), jnp.float32),
+            pltpu.VMEM((128, 512), jnp.float32),
+            pltpu.VMEM((128, 512), jnp.float32),
+            pltpu.VMEM((128, 128), jnp.float32),
+            pltpu.VMEM((128, 128), jnp.float32),
+            pltpu.VMEM((128, 128), jnp.float32),
+        ],
+        compiler_params=pltpu.CompilerParams(vmem_limit_bytes=16 * 2**20),
+        name="factor",
+    )(packed, sketch)
     core = pl.pallas_call(
         core_kernel,
         out_shape=jax.ShapeDtypeStruct((4, 512, 256), jnp.bfloat16),
         in_specs=[VMEM, VMEM],
-        out_specs=ANY,
+        out_specs=VMEM,
         scratch_shapes=[
             pltpu.VMEM((256, 256), jnp.bfloat16),
             pltpu.VMEM((128, 4096), jnp.bfloat16),
@@ -305,7 +412,7 @@
             DMA((GX * GY,)), DMA((GX * GY,)), DMA,
         ],
         compiler_params=pltpu.CompilerParams(
-            collective_id=1, has_side_effects=True, vmem_limit_bytes=40 * 2**20
+            collective_id=1, has_side_effects=True, vmem_limit_bytes=20 * 2**20
         ),
         name="core",
     )(factor_t, xs)

time: 164 us -> 113 us (0.69)
  other arithmetic: 46 us -> 0 us
  local copies, waits for them, and re-layouts: 9.02 us -> 0.98 us
  Pallas kernels: 104 us -> 111 us
  matrix products: 3.97 us -> 0 us
    another operation x10 -> x0, other arithmetic: 45.9 us -> none  [the longest x6 25 us: orthonormal(): lower = jnp.linalg.cholesky(inner)]
    unnamed x10 -> x3, local copies, waits for them, and re-layouts: 8.14 us -> 0.98 us
    pallas_call x0 -> x1, Pallas kernels: none -> 6.97 us  [shards(): pl.pallas_call(factor_kernel, out_shape=(jax.ShapeDtypeStruct((512, 128),...]
    dot_general x4 -> x0, matrix products: 3.14 us -> none  [the longest x2 1.96 us: orthonormal(): image = jnp.dot(gram, basis, precision=lax.Precision.HIGHEST)]
where the time goes in v3:
time: 113 us; the launch traced here: 112 us
  Pallas kernels  111 us (98%)
    pallas_call x1, Pallas kernels, shards(): pl.pallas_call(gram_kernel, out_shape=(jax.ShapeDtypeStruct((512, 4096),...  85.1 us
    pallas_call x1, Pallas kernels, shards(): pl.pallas_call(core_kernel, out_shape=jax.ShapeDtypeStruct((4, 512, 256),...  18.8 us
    pallas_call x1, Pallas kernels, shards(): pl.pallas_call(factor_kernel, out_shape=(jax.ShapeDtypeStruct((512, 128),...  6.97 us

profile of v3, /device:TPU:1, one launch (start us, length us, event | category | flops | bytes accessed | tf_op | source)
XLA Modules:
  0.0 112.5 jit_solution(11197157417507949936)
XLA Ops:
  0.6 0.0 copy-start
  0.6 85.1 %gram.1 = (bf16[512,4096]{1,0:T(8,128)(2,1)S(1)}, f32[1280,128]{1,0:T(8,128)S(1)}) custom-call(bf16[128,64,256]{2,1,0:T(8,128)(2,1)} %field.1), custom_call_target="tpu_custom_call" | custom-call | tf_op jit(solution)/shard_map/gram/pallas_call | solution.py:356
  85.7 0.0 copy-done
  85.7 7.0 %factor.1 = (f32[512,128]{1,0:T(8,128)}, bf16[128,512]{1,0:T(8,128)(2,1)S(1)}) custom-call(f32[1280,128]{1,0:T(8,128)S(1)} %get-tuple-element.6.packed, f32[512,128]{1,0:T(8,128)S(1)} %copy-done), custom_call_target="tpu_custom_call" | custom-call | tf_op jit(solution)/shard_map/factor/pallas_call | solution.py:384
  92.7 18.8 %core.1 = bf16[4,512,256]{2,1,0:T(8,128)(2,1)S(1)} custom-call(bf16[128,512]{1,0:T(8,128)(2,1)S(1)} %get-tuple-element.8.factor_t, bf16[512,4096]{1,0:T(8,128)(2,1)S(1)} %get-tuple-element.9.xs), custom_call_target="tpu_custom_call" | custom-call | tf_op jit(solution)/shard_map/core/pallas_call | solution.py:403
  111.5 1.0 copy.5
Async XLA Ops:
  0.6 85.1 %copy-start = (f32[512,128]{1,0:T(8,128)S(1)}, f32[512,128]{1,0:T(8,128)}, u32[]{:S(2)}) copy-start(f32[512,128]{1,0:T(8,128)} %sketch.1) | copy-start | bytes 786436

commit v4 on v3

--- a/solution.py
+++ b/solution.py
@@ -13,6 +13,7 @@
 YC = GY // 2
 PLANE = GX * YC
 SUB = 4
+FIRST = (0, 128, 384, 768)
 
 
 def remote(src, dst, send, recv, dev):
@@ -29,7 +30,7 @@
     return jnp.where(hit, 1.0, 0.0).astype(jnp.bfloat16)
 
 
-def gram_kernel(field, xs, gfin, raw, perm, gp, r1, acc, r2, r3, a_send, a_recv, own_sem,
+def gram_kernel(field, xs, gfin, raw, perm, gp, got, acc, r2e, r2l, r3e, r3l, a_send, a_recv, own_sem,
                 c_send, c_recv, p_send, p_recv, z_send, z_recv, g_send, g_recv, f_send, f_recv):
     x, y, z = lax.axis_index("gx"), lax.axis_index("gy"), lax.axis_index("gz")
     core, yc = lax.rem(y, 2), lax.div(y, 2)
@@ -55,8 +56,7 @@
     for dev in peers:
         pl.semaphore_signal(barrier, inc=1, device_id=dev, device_id_type=MESH)
 
-    rows = field.shape[0] // SUB
-    pieces = 16
+    rows, pieces = 32, 16
     mine = pltpu.make_async_copy(
         field.at[:, pl.ds(pl.multiple_of(x * pieces, pieces), pieces), :], raw.at[0], own_sem
     )
@@ -65,121 +65,144 @@
     pl.semaphore_wait(barrier, len(peers))
 
     sends = {}
-    for d in (1, 3, 2):
-        to = lax.rem(x + d, GX)
-        for s in range(SUB):
+    for s in range(SUB):
+        for d in (2, 1, 3):
+            to = lax.rem(x + d, GX)
             sends[d, s] = remote(
                 field.at[pl.ds(s * rows, rows), pl.ds(pl.multiple_of(to * pieces, pieces), pieces), :],
                 raw.at[GX - d, pl.ds(s * rows, rows)],
                 a_send.at[d * SUB + s], a_recv.at[(GX - d) * SUB + s], xdev(d),
             )
-            sends[d, s].start()
+            if s < 2:
+                sends[d, s].start()
 
     def relayout(d, s):
-        base = pl.multiple_of(lax.rem(x + d, GX) * 128, 128)
-
-        def group(g, carry):
-            i0 = s * rows + g * 16
-            block = raw[d, pl.ds(i0, 16)].reshape(256, 256)
+        base = s * 128 + lax.rem(x + d, GX) * rows
+
+        for g in range(rows // 16):
+            block = raw[d, s * rows + g * 16:s * rows + g * 16 + 16].reshape(256, 256)
             out = jnp.dot(perm[...], block, preferred_element_type=jnp.float32).astype(jnp.bfloat16)
             for j in range(16):
-                xs[pl.ds(pl.multiple_of(base + i0, 16), 16), j * 256:(j + 1) * 256] = out[j * 16:(j + 1) * 16]
-            return carry
-
-        lax.fori_loop(0, rows // 16, group, 0)
-
-    def block(a, b, pos):
-        def part(k, total):
-            k0 = pl.multiple_of(k * 1024, 1024)
-            u = xs[pl.ds(pl.multiple_of(a * 128, 128), 128), pl.ds(k0, 1024)]
-            v = xs[pl.ds(pl.multiple_of(b * 128, 128), 128), pl.ds(k0, 1024)]
-            return total + lax.dot_general(u, v, (((1,), (1,)), ((), ())), preferred_element_type=jnp.float32)
-
-        out = lax.fori_loop(0, 4, part, jnp.zeros((128, 128), jnp.float32))
-        gp[pl.ds(pl.multiple_of(pos * 128, 128), 128), :] = out
+                xs[pl.ds(pl.multiple_of(base + g * 16, 16), 16), j * 256:(j + 1) * 256] = out[j * 16:(j + 1) * 16]
+
+    def products(s):
+        n = 128 * (s + 1)
+        at = slice(FIRST[s], FIRST[s] + n)
+        for k in range(4):
+            cols = slice(k * 1024, (k + 1) * 1024)
+            part = lax.dot_general(
+                xs[0:n, cols], xs[s * 128:(s + 1) * 128, cols], (((1,), (1,)), ((), ())),
+                preferred_element_type=jnp.float32,
+            )
+            gp[at, :] = part if k == 0 else gp[at, :] + part
+
+    me = pnum(0)
+    order = [10, 2, 8, 6, 9, 11, 14, 1, 3, 4, 12, 5, 7, 13, 15]
+    pending = []
+
+    def start(copy):
+        copy.start()
+        pending.append(copy)
+        return copy
+
+    class Sum:
+        def __init__(self, n, lo, size, r2, r3):
+            self.n, self.lo, self.half, self.piece = n, lo, size // 2, size // 2 // PLANE
+            self.r2, self.r3 = r2, r3
+
+        def mine(self, which, q=0, size=None):
+            first = self.lo + which * self.half + q * self.piece
+            return pl.ds(pl.multiple_of(first, 8), self.half if size is None else size)
+
+        def to_core(self):
+            self.swap = start(remote(
+                gp.at[self.mine(1 - core)], got.at[pl.ds(self.lo // 2, self.half)],
+                c_send.at[self.n], c_recv.at[self.n], other,
+            ))
+
+        def from_core(self):
+            self.swap.wait_recv()
+            here = slice(self.lo // 2, self.lo // 2 + self.half)
+            acc[here] = gp[self.mine(core)] + got[here]
+
+        def part(self, q):
+            return pl.ds(pl.multiple_of(self.lo // 2 + q * self.piece, 8), self.piece)
+
+        def to_plane(self):
+            for d in order:
+                start(remote(acc.at[self.part(pnum(d))], self.r2.at[me], p_send.at[self.n, d], p_recv.at[self.n, d], pdev(d)))
+            self.r2[me] = acc[self.part(me)]
+
+        def from_plane(self):
+            for d in order:
+                at = self.r2.at[pfrom(d)]
+                remote(at, at, p_send.at[self.n, d], p_recv.at[self.n, d], pdev(d)).wait_recv()
+            self.r3[z] = total_of([self.r2[q] for q in range(PLANE)])
+
+        def to_line(self):
+            for d in (4, 3, 5, 2, 6, 1, 7):
+                start(remote(self.r3.at[z], self.r3.at[z], z_send.at[self.n, d], z_recv.at[self.n, d], zdev(d)))
+
+        def from_line(self):
+            for d in (1, 7, 2, 6, 3, 5, 4):
+                at = self.r3.at[lax.rem(z - d + GZ, GZ)]
+                remote(at, at, z_send.at[self.n, d], z_recv.at[self.n, d], zdev(d)).wait_recv()
+            gfin[self.mine(core, me, self.piece)] = total_of([self.r3[q] for q in range(GZ)])
+
+        def place(self, which, q):
+            return gfin.at[self.mine(which, q, self.piece)]
+
+        def spread(self):
+            at = self.place(core, me)
+            for d in order:
+                start(remote(at, at, g_send.at[self.n, d], g_recv.at[self.n, d], pdev(d)))
+            start(remote(at, at, f_send.at[self.n, 0], f_recv.at[self.n, 0], other))
+
+        def gather(self):
+            for d in order[::-1]:
+                at = self.place(core, pfrom(d))
+                remote(at, at, g_send.at[self.n, d], g_recv.at[self.n, d], pdev(d)).wait_recv()
+                start(remote(at, at, f_send.at[self.n, d], f_recv.at[self.n, d], other))
+
+        def finish(self):
+            for d in range(PLANE):
+                at = self.place(1 - core, pfrom(d))
+                remote(at, at, f_send.at[self.n, d], f_recv.at[self.n, d], other).wait_recv()
+
+    early, late = Sum(0, 0, 768, r2e, r3e), Sum(1, 768, 512, r2l, r3l)
 
     mine.wait()
     for s in range(SUB):
         relayout(0, s)
-    m1, p1, p2 = lax.rem(x + 3, GX), lax.rem(x + 1, GX), lax.rem(x + 2, GX)
-    block(x, x, x)
-    for d in (1, 3):
-        for s in range(SUB):
+    for s in range(SUB):
+        for d in (1, 3, 2):
             sends[GX - d, s].wait_recv()
+            if s + 2 < SUB:
+                sends[GX - d, s + 2].start()
             relayout(d, s)
-    block(p1, p1, p1)
-    block(m1, m1, m1)
-    block(x, p1, 4 + x)
-    block(m1, x, 4 + m1)
-    odd = lax.rem(x + 1, 2)
-    block(odd, odd + 2, 8 + odd)
-    for s in range(SUB):
-        sends[2, s].wait_recv()
-        relayout(2, s)
-    block(p2, p2, p2)
-    block(p1, p2, 4 + p1)
-    block(p2, m1, 4 + p2)
-    even = lax.rem(x, 2)
-    block(even, even + 2, 8 + even)
-
-    half = 640
-    to_other = remote(gp.at[pl.ds(pl.multiple_of((1 - core) * half, half), half)], r1, c_send, c_recv, other)
-    to_other.start()
-    to_other.wait_recv()
-    acc[...] = gp[pl.ds(pl.multiple_of(core * half, half), half)] + r1[...]
-
-    piece = half // PLANE
-    me = pnum(0)
-    order = [10, 2, 8, 6, 9, 11, 14, 1, 3, 4, 12, 5, 7, 13, 15]
-    plane = {}
-    for d in order:
-        plane[d] = remote(
-            acc.at[pl.ds(pl.multiple_of(pnum(d) * piece, 8), piece)], r2.at[me],
-            p_send.at[d], p_recv.at[d], pdev(d),
-        )
-        plane[d].start()
-    r2[me] = acc[pl.ds(pl.multiple_of(me * piece, 8), piece)]
-    for d in order:
-        remote(r2.at[pfrom(d)], r2.at[pfrom(d)], p_send.at[d], p_recv.at[d], pdev(d)).wait_recv()
-    total = r2[0]
-    for q in range(1, PLANE):
-        total = total + r2[q]
-    r3[z] = total
-
-    along = {}
-    for d in (4, 3, 5, 2, 6, 1, 7):
-        along[d] = remote(r3.at[z], r3.at[z], z_send.at[d], z_recv.at[d], zdev(d))
-        along[d].start()
-    for d in (1, 7, 2, 6, 3, 5, 4):
-        src = lax.rem(z - d + GZ, GZ)
-        remote(r3.at[src], r3.at[src], z_send.at[d], z_recv.at[d], zdev(d)).wait_recv()
-    total = r3[0]
-    for q in range(1, GZ):
-        total = total + r3[q]
-
-    def place(q):
-        return gfin.at[pl.ds(pl.multiple_of(core * half + q * piece, 8), piece)]
-
-    gfin[pl.ds(pl.multiple_of(core * half + me * piece, 8), piece)] = total
-    spread = {}
-    for d in order:
-        spread[d] = remote(place(me), place(me), g_send.at[d], g_recv.at[d], pdev(d))
-        spread[d].start()
-    onward = {0: remote(place(me), place(me), f_send.at[0], f_recv.at[0], other)}
-    onward[0].start()
-    for d in order[::-1]:
-        at = place(pfrom(d))
-        remote(at, at, g_send.at[d], g_recv.at[d], pdev(d)).wait_recv()
-        onward[d] = remote(at, at, f_send.at[d], f_recv.at[d], other)
-        onward[d].start()
-    for d in range(PLANE):
-        there = gfin.at[pl.ds(pl.multiple_of((1 - core) * half + pfrom(d) * piece, 8), piece)]
-        remote(there, there, f_send.at[d], f_recv.at[d], other).wait_recv()
-
-    for copies in (sends, plane, along, spread, onward):
-        for c in copies.values():
-            c.wait_send()
-    to_other.wait_send()
+        if s == 3:
+            early.to_plane()
+        products(s)
+        if s == 2:
+            early.to_core()
+            early.from_core()
+    late.to_core()
+    late.from_core()
+    late.to_plane()
+    early.from_plane()
+    early.to_line()
+    late.from_plane()
+    late.to_line()
+    early.from_line()
+    early.spread()
+    late.from_line()
+    late.spread()
+    early.gather()
+    late.gather()
+    early.finish()
+    late.finish()
+    for c in list(sends.values()) + pending:
+        c.wait_send()
 
 
 def core_kernel(factor_t, xs, out, perm, t, buf, send, recv, own_sem):
@@ -194,38 +217,28 @@
         pl.semaphore_signal(barrier, inc=1, device_id=dev(dx, dy), device_id_type=MESH)
     perm[...] = swap16()
 
-    def product(j, carry):
-        cols = pl.ds(pl.multiple_of(j * 256, 256), 256)
+    for j in range(16):
+        cols = slice(j * 256, (j + 1) * 256)
         t[:, cols] = jnp.dot(factor_t[...], xs[:, cols], preferred_element_type=jnp.float32).astype(jnp.bfloat16)
-        return carry
-
-    lax.fori_loop(0, 16, product, 0)
+    for r0 in range(0, 128, 16):
+        block = jnp.concatenate([t[r0:r0 + 16, j * 256:(j + 1) * 256] for j in range(16)], axis=0)
+        rows = jnp.dot(perm[...], block, preferred_element_type=jnp.float32).astype(jnp.bfloat16)
+        buf[r0:r0 + 16] = rows.reshape(16, 16, 256)
     pl.semaphore_wait(barrier, len(offsets) - 1)
 
     def place(px, py):
         return out.at[:, pl.ds(pl.multiple_of(py * 64 + px * 16, 16), 16), :]
 
     copies = {}
-    for dx in (2, 1, 3, 0):
-        to = lax.rem(x + dx, GX)
-
-        def group(g, carry):
-            r0 = pl.multiple_of(to * 32 + g * 16, 16)
-            block = jnp.concatenate([t[pl.ds(r0, 16), j * 256:(j + 1) * 256] for j in range(16)], axis=0)
-            rows = jnp.dot(perm[...], block, preferred_element_type=jnp.float32).astype(jnp.bfloat16)
-            buf[pl.ds(r0, 16)] = rows.reshape(16, 16, 256)
-            return carry
-
-        lax.fori_loop(0, 2, group, 0)
-        for k, dy in enumerate((4, 5, 3, 2, 6, 7, 1, 0)):
-            src = buf.at[pl.ds(to * 32 + lax.rem(y + dy, GY) * 4, 4)]
-            if dx or dy:
-                n = dx * GY + dy
-                copies[n] = remote(src, place(x, y), send.at[n], recv.at[n], dev(dx, dy))
-                copies[n].start()
-            else:
-                mine = pltpu.make_async_copy(src, place(x, y), own_sem)
-                mine.start()
+    for dx, dy in offsets:
+        src = buf.at[pl.ds(lax.rem(x + dx, GX) * 32 + lax.rem(y + dy, GY) * 4, 4)]
+        if dx or dy:
+            n = dx * GY + dy
+            copies[n] = remote(src, place(x, y), send.at[n], recv.at[n], dev(dx, dy))
+            copies[n].start()
+        else:
+            mine = pltpu.make_async_copy(src, place(x, y), own_sem)
+            mine.start()
     for dx, dy in offsets[:-1]:
         n = dx * GY + dy
         at = place(lax.rem(x - dx + GX, GX), lax.rem(y - dy + GY, GY))
@@ -296,21 +309,15 @@
 
 
 def factor_kernel(packed, sketch, factor, factor_t, gram, basis, image, a, d, diagonal):
-    def block(k):
-        return packed[128 * k:128 * k + 128, :]
-
-    def put(i, j, value):
-        gram[128 * i:128 * i + 128, 128 * j:128 * j + 128] = value
-
-    for k in range(4):
-        put(k, k, block(k))
-        n = (k + 1) % 4
-        put(k, n, block(4 + k))
-        put(n, k, block(4 + k).T)
-    for k in range(2):
-        put(k, k + 2, block(8 + k))
-        put(k + 2, k, block(8 + k).T)
-    start = sketch[...].T
+    for s in range(SUB):
+        for r in range(s + 1):
+            block = packed[FIRST[s] + 128 * r:FIRST[s] + 128 * r + 128, :]
+            gram[128 * r:128 * r + 128, 128 * s:128 * s + 128] = block
+            if r < s:
+                gram[128 * s:128 * s + 128, 128 * r:128 * r + 128] = block.T
+    start = jnp.concatenate(
+        [sketch[128 * b + 32 * s:128 * b + 32 * s + 32, :] for s in range(SUB) for b in range(GX)], axis=0
+    ).T
     row = lax.broadcasted_iota(jnp.int32, (128, 128), 0)
     col = lax.broadcasted_iota(jnp.int32, (128, 128), 1)
 
@@ -324,7 +331,10 @@
 
     def finish():
         factor_t[...] = basis[...].astype(jnp.bfloat16)
-        factor[...] = basis[...].T
+        final = basis[...].T
+        for s in range(SUB):
+            for b in range(GX):
+                factor[128 * b + 32 * s:128 * b + 32 * s + 32, :] = final[128 * s + 32 * b:128 * s + 32 * b + 32, :]
 
     first = exact_dot(start, gram[...])
     first = first * lax.rsqrt(jnp.sum(first * first, axis=1, keepdims=True))
@@ -367,14 +377,16 @@
             pltpu.VMEM((1280, 128), jnp.float32),
             pltpu.VMEM((640, 128), jnp.float32),
             pltpu.VMEM((640, 128), jnp.float32),
-            pltpu.VMEM((PLANE, 40, 128), jnp.float32),
-            pltpu.VMEM((GZ, 40, 128), jnp.float32),
+            pltpu.VMEM((PLANE, 24, 128), jnp.float32),
+            pltpu.VMEM((PLANE, 16, 128), jnp.float32),
+            pltpu.VMEM((GZ, 24, 128), jnp.float32),
+            pltpu.VMEM((GZ, 16, 128), jnp.float32),
             DMA((GX * SUB,)), DMA((GX * SUB,)), DMA,
-            DMA, DMA,
-            DMA((PLANE,)), DMA((PLANE,)),
-            DMA((GZ,)), DMA((GZ,)),
-            DMA((PLANE,)), DMA((PLANE,)),
-            DMA((PLANE,)), DMA((PLANE,)),
+            DMA((2,)), DMA((2,)),
+            DMA((2, PLANE)), DMA((2, PLANE)),
+            DMA((2, GZ)), DMA((2, GZ)),
+            DMA((2, PLANE)), DMA((2, PLANE)),
+            DMA((2, PLANE)), DMA((2, PLANE)),
         ],
         compiler_params=pltpu.CompilerParams(
             collective_id=0, has_side_effects=True, vmem_limit_bytes=24 * 2**20

time: 113 us -> 105 us (0.929)
  Pallas kernels: 111 us -> 103 us
    pallas_call x1, Pallas kernels: 85.1 us -> 78.7 us  [shards(): pl.pallas_call(gram_kernel, out_shape=(jax.ShapeDtypeStruct((512, 4096),...]
    pallas_call x1, Pallas kernels: 18.8 us -> 17.2 us  [shards(): pl.pallas_call(core_kernel, out_shape=jax.ShapeDtypeStruct((4, 512, 256),...]
where the time goes in v4:
time: 105 us; the launch traced here: 104 us
  Pallas kernels  103 us (98%)
    pallas_call x1, Pallas kernels, shards(): pl.pallas_call(gram_kernel, out_shape=(jax.ShapeDtypeStruct((512, 4096),...  78.7 us
    pallas_call x1, Pallas kernels, shards(): pl.pallas_call(core_kernel, out_shape=jax.ShapeDtypeStruct((4, 512, 256),...  17.2 us
    pallas_call x1, Pallas kernels, shards(): pl.pallas_call(factor_kernel, out_shape=(jax.ShapeDtypeStruct((512, 128),...  6.98 us

profile of v4, /device:TPU:1, one launch (start us, length us, event | category | flops | bytes accessed | tf_op | source)
XLA Modules:
  0.0 104.5 jit_solution(3119309393821166662)
XLA Ops:
  0.6 0.0 copy-start
  0.6 78.7 %gram.1 = (bf16[512,4096]{1,0:T(8,128)(2,1)S(1)}, f32[1280,128]{1,0:T(8,128)S(1)}) custom-call(bf16[128,64,256]{2,1,0:T(8,128)(2,1)} %field.1), custom_call_target="tpu_custom_call" | custom-call | tf_op jit(solution)/shard_map/gram/pallas_call | solution.py:366
  79.3 0.0 copy-done
  79.3 7.0 %factor.1 = (f32[512,128]{1,0:T(8,128)}, bf16[128,512]{1,0:T(8,128)(2,1)S(1)}) custom-call(f32[1280,128]{1,0:T(8,128)S(1)} %get-tuple-element.6.packed, f32[512,128]{1,0:T(8,128)S(1)} %copy-done), custom_call_target="tpu_custom_call" | custom-call | tf_op jit(solution)/shard_map/factor/pallas_call | solution.py:396
  86.3 17.2 %core.1 = bf16[4,512,256]{2,1,0:T(8,128)(2,1)S(1)} custom-call(bf16[128,512]{1,0:T(8,128)(2,1)S(1)} %get-tuple-element.8.factor_t, bf16[512,4096]{1,0:T(8,128)(2,1)S(1)} %get-tuple-element.9.xs), custom_call_target="tpu_custom_call" | custom-call | tf_op jit(solution)/shard_map/core/pallas_call | solution.py:415
  103.5 1.0 copy.5
Async XLA Ops:
  0.6 78.7 %copy-start = (f32[512,128]{1,0:T(8,128)S(1)}, f32[512,128]{1,0:T(8,128)}, u32[]{:S(2)}) copy-start(f32[512,128]{1,0:T(8,128)} %sketch.1) | copy-start | bytes 786436

commit v5 on v4

--- a/solution.py
+++ b/solution.py
@@ -52,17 +52,12 @@
         return lax.rem(x - d // YC + GX, GX) * YC + lax.rem(yc - d % YC + YC, YC)
 
     barrier = pltpu.get_barrier_semaphore()
-    peers = [pdev(d) for d in range(1, PLANE)] + [zdev(d) for d in range(1, GZ)] + [other]
-    for dev in peers:
+    peers = [pdev(d) for d in (8, 4, 12, 10, 2, 6, 9, 11, 14, 1, 3, 5, 7, 13, 15)] + [zdev(d) for d in (4, 3, 5, 2, 6, 1, 7)]
+    for dev in peers + [other]:
         pl.semaphore_signal(barrier, inc=1, device_id=dev, device_id_type=MESH)
 
     rows, pieces = 32, 16
-    mine = pltpu.make_async_copy(
-        field.at[:, pl.ds(pl.multiple_of(x * pieces, pieces), pieces), :], raw.at[0], own_sem
-    )
-    mine.start()
-    perm[...] = swap16()
-    pl.semaphore_wait(barrier, len(peers))
+    pl.semaphore_wait(barrier, len(peers) + 1)
 
     sends = {}
     for s in range(SUB):
@@ -75,6 +70,11 @@
             )
             if s < 2:
                 sends[d, s].start()
+    mine = pltpu.make_async_copy(
+        field.at[:, pl.ds(pl.multiple_of(x * pieces, pieces), pieces), :], raw.at[0], own_sem
+    )
+    mine.start()
+    perm[...] = swap16()
 
     def relayout(d, s):
         base = s * 128 + lax.rem(x + d, GX) * rows
@@ -105,6 +105,10 @@
         pending.append(copy)
         return copy
 
+    def settle():
+        while pending:
+            pending.pop(0).wait_send()
+
     class Sum:
         def __init__(self, n, lo, size, r2, r3):
             self.n, self.lo, self.half, self.piece = n, lo, size // 2, size // 2 // PLANE
@@ -156,18 +160,25 @@
             at = self.place(core, me)
             for d in order:
                 start(remote(at, at, g_send.at[self.n, d], g_recv.at[self.n, d], pdev(d)))
-            start(remote(at, at, f_send.at[self.n, 0], f_recv.at[self.n, 0], other))
+
+        def row(self, which, dx):
+            first = self.lo + which * self.half + lax.rem(x - dx + GX, GX) * YC * self.piece
+            return gfin.at[pl.ds(pl.multiple_of(first, 8), YC * self.piece)]
 
         def gather(self):
-            for d in order[::-1]:
-                at = self.place(core, pfrom(d))
-                remote(at, at, g_send.at[self.n, d], g_recv.at[self.n, d], pdev(d)).wait_recv()
-                start(remote(at, at, f_send.at[self.n, d], f_recv.at[self.n, d], other))
+            for dx in (0, 1, 3, 2):
+                for dy in range(YC):
+                    d = dx * YC + dy
+                    if d:
+                        at = self.place(core, pfrom(d))
+                        remote(at, at, g_send.at[self.n, d], g_recv.at[self.n, d], pdev(d)).wait_recv()
+                at = self.row(core, dx)
+                start(remote(at, at, f_send.at[self.n, dx], f_recv.at[self.n, dx], other))
 
         def finish(self):
-            for d in range(PLANE):
-                at = self.place(1 - core, pfrom(d))
-                remote(at, at, f_send.at[self.n, d], f_recv.at[self.n, d], other).wait_recv()
+            for dx in (0, 1, 3, 2):
+                at = self.row(1 - core, dx)
+                remote(at, at, f_send.at[self.n, dx], f_recv.at[self.n, dx], other).wait_recv()
 
     early, late = Sum(0, 0, 768, r2e, r3e), Sum(1, 768, 512, r2l, r3l)
 
@@ -180,8 +191,8 @@
             if s + 2 < SUB:
                 sends[GX - d, s + 2].start()
             relayout(d, s)
-        if s == 3:
-            early.to_plane()
+            if s == 3 and d == 1:
+                early.to_plane()
         products(s)
         if s == 2:
             early.to_core()
@@ -195,26 +206,40 @@
     late.to_line()
     early.from_line()
     early.spread()
+    for c in sends.values():
+        c.wait_send()
+    settle()
     late.from_line()
     late.spread()
     early.gather()
+    early.finish()
+    settle()
     late.gather()
-    early.finish()
+    settle()
     late.finish()
-    for c in list(sends.values()) + pending:
-        c.wait_send()
-
-
-def core_kernel(factor_t, xs, out, perm, t, buf, send, recv, own_sem):
+
+
+def core_kernel(factor_t, xs, out, perm, t, buf, send, recv, own_sem, ready):
     x, y, z = lax.axis_index("gx"), lax.axis_index("gy"), lax.axis_index("gz")
-
-    def dev(dx, dy):
-        return (lax.rem(x + dx, GX), lax.rem(y + dy, GY), z)
-
-    offsets = [(dx, dy) for dx in (2, 1, 3, 0) for dy in (4, 5, 3, 2, 6, 7, 1, 0)]
+    core, yc = lax.rem(y, 2), lax.div(y, 2)
+
+    def there(dx, dy, f):
+        flip = 1 - core if f else core
+        return lax.rem(x + dx + GX, GX), 2 * lax.rem(yc + dy + YC, YC) + flip
+
+    def dev(dx, dy, f):
+        return (*there(dx, dy, f), z)
+
+    def hops(dx, dy):
+        return min(dx, GX - dx) + min(dy, YC - dy)
+
+    offsets = [(dx, dy, f) for dx in range(GX) for dy in range(YC) for f in range(2) if dx or dy or f]
+    near = sorted((o for o in offsets if hops(*o[:2]) <= 2), key=lambda o: -hops(*o[:2]))
+    far = sorted((o for o in offsets if hops(*o[:2]) > 2), key=lambda o: -hops(*o[:2]))
+    corners = [dev(1, 1, 0), dev(3, 3, 0)]
     barrier = pltpu.get_barrier_semaphore()
-    for dx, dy in offsets[:-1]:
-        pl.semaphore_signal(barrier, inc=1, device_id=dev(dx, dy), device_id_type=MESH)
+    for o in near:
+        pl.semaphore_signal(barrier, inc=1, device_id=dev(*o), device_id_type=MESH)
     perm[...] = swap16()
 
     for j in range(16):
@@ -224,27 +249,38 @@
         block = jnp.concatenate([t[r0:r0 + 16, j * 256:(j + 1) * 256] for j in range(16)], axis=0)
         rows = jnp.dot(perm[...], block, preferred_element_type=jnp.float32).astype(jnp.bfloat16)
         buf[r0:r0 + 16] = rows.reshape(16, 16, 256)
-    pl.semaphore_wait(barrier, len(offsets) - 1)
+    pl.semaphore_wait(barrier, len(near))
+    for corner in corners:
+        pl.semaphore_signal(ready, inc=1, device_id=corner, device_id_type=MESH)
 
     def place(px, py):
         return out.at[:, pl.ds(pl.multiple_of(py * 64 + px * 16, 16), 16), :]
 
-    copies = {}
-    for dx, dy in offsets:
-        src = buf.at[pl.ds(lax.rem(x + dx, GX) * 32 + lax.rem(y + dy, GY) * 4, 4)]
-        if dx or dy:
-            n = dx * GY + dy
-            copies[n] = remote(src, place(x, y), send.at[n], recv.at[n], dev(dx, dy))
-            copies[n].start()
-        else:
-            mine = pltpu.make_async_copy(src, place(x, y), own_sem)
-            mine.start()
-    for dx, dy in offsets[:-1]:
-        n = dx * GY + dy
-        at = place(lax.rem(x - dx + GX, GX), lax.rem(y - dy + GY, GY))
-        remote(at, at, send.at[n], recv.at[n], dev(dx, dy)).wait_recv()
-    for c in copies.values():
+    def number(dx, dy, f):
+        return (dx * YC + dy) * 2 + f
+
+    copies = []
+
+    def push(o):
+        px, py = there(*o)
+        src = buf.at[pl.ds(px * 32 + py * 4, 4)]
+        copies.append(remote(src, place(x, y), send.at[number(*o)], recv.at[number(*o)], dev(*o)))
+        copies[-1].start()
+
+    two = [o for o in near if hops(*o[:2]) == 2]
+    for o in two:
+        push(o)
+    pl.semaphore_wait(ready, len(corners))
+    for o in far + near[len(two):]:
+        push(o)
+    mine = pltpu.make_async_copy(buf.at[pl.ds(x * 32 + y * 4, 4)], place(x, y), own_sem)
+    mine.start()
+    for c in copies:
         c.wait_send()
+    for dx, dy, f in near + far:
+        at = place(*there(-dx, -dy, f))
+        n = number(dx, dy, f)
+        remote(at, at, send.at[n], recv.at[n], dev(dx, dy, f)).wait_recv()
     mine.wait()
 
 
@@ -386,7 +422,7 @@
             DMA((2, PLANE)), DMA((2, PLANE)),
             DMA((2, GZ)), DMA((2, GZ)),
             DMA((2, PLANE)), DMA((2, PLANE)),
-            DMA((2, PLANE)), DMA((2, PLANE)),
+            DMA((2, GX)), DMA((2, GX)),
         ],
         compiler_params=pltpu.CompilerParams(
             collective_id=0, has_side_effects=True, vmem_limit_bytes=24 * 2**20
@@ -422,6 +458,7 @@
             pltpu.VMEM((128, 4096), jnp.bfloat16),
             pltpu.VMEM((128, 16, 256), jnp.bfloat16),
             DMA((GX * GY,)), DMA((GX * GY,)), DMA,
+            pltpu.SemaphoreType.REGULAR,
         ],
         compiler_params=pltpu.CompilerParams(
             collective_id=1, has_side_effects=True, vmem_limit_bytes=20 * 2**20

time: 105 us -> 104 us (level)
  no operation moved by 1% of the time
where the time goes in v5:
time: 104 us
  Pallas kernels  103 us (99%)
    pallas_call x1, Pallas kernels, shards(): pl.pallas_call(gram_kernel, out_shape=(jax.ShapeDtypeStruct((512, 4096),...  78.7 us
    pallas_call x1, Pallas kernels, shards(): pl.pallas_call(core_kernel, out_shape=jax.ShapeDtypeStruct((4, 512, 256),...  17 us
    pallas_call x1, Pallas kernels, shards(): pl.pallas_call(factor_kernel, out_shape=(jax.ShapeDtypeStruct((512, 128),...  6.98 us

profile of v5, /device:TPU:1, one launch (start us, length us, event | category | flops | bytes accessed | tf_op | source)
XLA Modules:
  0.0 104.3 jit_solution(8901464247357268153)
XLA Ops:
  0.6 0.0 copy-start
  0.6 78.7 %gram.1 = (bf16[512,4096]{1,0:T(8,128)(2,1)S(1)}, f32[1280,128]{1,0:T(8,128)S(1)}) custom-call(bf16[128,64,256]{2,1,0:T(8,128)(2,1)} %field.1), custom_call_target="tpu_custom_call" | custom-call | tf_op jit(solution)/shard_map/gram/pallas_call | solution.py:402
  79.3 0.0 copy-done
  79.3 7.0 %factor.1 = (f32[512,128]{1,0:T(8,128)}, bf16[128,512]{1,0:T(8,128)(2,1)S(1)}) custom-call(f32[1280,128]{1,0:T(8,128)S(1)} %get-tuple-element.6.packed, f32[512,128]{1,0:T(8,128)S(1)} %copy-done), custom_call_target="tpu_custom_call" | custom-call | tf_op jit(solution)/shard_map/factor/pallas_call | solution.py:432
  86.3 17.0 %core.1 = bf16[4,512,256]{2,1,0:T(8,128)(2,1)S(1)} custom-call(bf16[128,512]{1,0:T(8,128)(2,1)S(1)} %get-tuple-element.8.factor_t, bf16[512,4096]{1,0:T(8,128)(2,1)S(1)} %get-tuple-element.9.xs), custom_call_target="tpu_custom_call" | custom-call | tf_op jit(solution)/shard_map/core/pallas_call | solution.py:451
  103.3 1.0 copy.5
Async XLA Ops:
  0.6 78.7 %copy-start = (f32[512,128]{1,0:T(8,128)S(1)}, f32[512,128]{1,0:T(8,128)}, u32[]{:S(2)}) copy-start(f32[512,128]{1,0:T(8,128)} %sketch.1) | copy-start | bytes 786436

commit v6 on v5

--- a/solution.py
+++ b/solution.py
@@ -12,8 +12,13 @@
 GX, GY, GZ = 4, 8, 8
 YC = GY // 2
 PLANE = GX * YC
-SUB = 4
-FIRST = (0, 128, 384, 768)
+LENGTH = (32, 32, 32, 16, 16)
+START = (0, 32, 64, 96, 112)
+BASE = (0, 128, 256, 384, 448)
+LAST = 4
+FIRST = (0, 128, 384, 768, 1024)
+PARTS = ((0, (0, 1)), (1, (0, 1)), (2, (0, 1)), (3, (0, 1)), (4, (0,)), (4, (1,)))
+AHEAD = 6
 
 
 def remote(src, dst, send, recv, dev):
@@ -56,45 +61,59 @@
     for dev in peers + [other]:
         pl.semaphore_signal(barrier, inc=1, device_id=dev, device_id_type=MESH)
 
-    rows, pieces = 32, 16
+    pieces = 16
     pl.semaphore_wait(barrier, len(peers) + 1)
 
     sends = {}
-    for s in range(SUB):
+    for m, (k, halves) in enumerate(PARTS):
+        rows = pl.ds(START[k], LENGTH[k])
+        cols = pl.ds(halves[0] * 128, len(halves) * 128)
         for d in (2, 1, 3):
             to = lax.rem(x + d, GX)
-            sends[d, s] = remote(
-                field.at[pl.ds(s * rows, rows), pl.ds(pl.multiple_of(to * pieces, pieces), pieces), :],
-                raw.at[GX - d, pl.ds(s * rows, rows)],
-                a_send.at[d * SUB + s], a_recv.at[(GX - d) * SUB + s], xdev(d),
+            sends[d, m] = remote(
+                field.at[rows, pl.ds(pl.multiple_of(to * pieces, pieces), pieces), cols],
+                raw.at[GX - d, rows, :, cols],
+                a_send.at[d * len(PARTS) + m], a_recv.at[(GX - d) * len(PARTS) + m], xdev(d),
             )
-            if s < 2:
-                sends[d, s].start()
+            if m < AHEAD:
+                sends[d, m].start()
     mine = pltpu.make_async_copy(
         field.at[:, pl.ds(pl.multiple_of(x * pieces, pieces), pieces), :], raw.at[0], own_sem
     )
     mine.start()
     perm[...] = swap16()
 
-    def relayout(d, s):
-        base = s * 128 + lax.rem(x + d, GX) * rows
-
-        for g in range(rows // 16):
-            block = raw[d, s * rows + g * 16:s * rows + g * 16 + 16].reshape(256, 256)
+    def relayout(d, m):
+        k, halves = PARTS[m]
+        base = BASE[k] + lax.rem(x + d, GX) * LENGTH[k]
+        for g in range(0, LENGTH[k], 16):
+            block = raw[d, START[k] + g:START[k] + g + 16, :, halves[0] * 128:halves[-1] * 128 + 128]
+            block = block.reshape(256, 128 * len(halves))
             out = jnp.dot(perm[...], block, preferred_element_type=jnp.float32).astype(jnp.bfloat16)
-            for j in range(16):
-                xs[pl.ds(pl.multiple_of(base + g * 16, 16), 16), j * 256:(j + 1) * 256] = out[j * 16:(j + 1) * 16]
-
-    def products(s):
-        n = 128 * (s + 1)
-        at = slice(FIRST[s], FIRST[s] + n)
-        for k in range(4):
-            cols = slice(k * 1024, (k + 1) * 1024)
+            for n, h in enumerate(halves):
+                for j in range(16):
+                    xs[pl.ds(pl.multiple_of(base + g, 16), 16), h * 2048 + j * 128:h * 2048 + j * 128 + 128] = (
+                        out[j * 16:(j + 1) * 16, n * 128:(n + 1) * 128]
+                    )
+
+    left_lanes = lax.broadcasted_iota(jnp.int32, (1, 128), 1) < 64
+
+    def products(m):
+        k, halves = PARTS[m]
+        wide = 4 * LENGTH[k]
+        n = BASE[k] + wide
+        for step in range(2 * halves[0], 2 * halves[-1] + 2):
+            cols = slice(step * 1024, (step + 1) * 1024)
+            right = xs[BASE[k]:n, cols]
+            if wide == 64:
+                right = jnp.concatenate([right, right], axis=0)
             part = lax.dot_general(
-                xs[0:n, cols], xs[s * 128:(s + 1) * 128, cols], (((1,), (1,)), ((), ())),
-                preferred_element_type=jnp.float32,
+                xs[0:n, cols], right, (((1,), (1,)), ((), ())), preferred_element_type=jnp.float32
             )
-            gp[at, :] = part if k == 0 else gp[at, :] + part
+            if wide == 64:
+                part = jnp.where(left_lanes, part[:n // 2], part[n // 2:])
+            at = slice(FIRST[k], FIRST[k] + part.shape[0])
+            gp[at, :] = part if step == 0 else gp[at, :] + part
 
     me = pnum(0)
     order = [10, 2, 8, 6, 9, 11, 14, 1, 3, 4, 12, 5, 7, 13, 15]
@@ -181,22 +200,22 @@
                 remote(at, at, f_send.at[self.n, dx], f_recv.at[self.n, dx], other).wait_recv()
 
     early, late = Sum(0, 0, 768, r2e, r3e), Sum(1, 768, 512, r2l, r3l)
+    gp[992:1024, :] = jnp.zeros((32, 128), jnp.float32)
 
     mine.wait()
-    for s in range(SUB):
-        relayout(0, s)
-    for s in range(SUB):
+    for m in range(len(PARTS)):
+        relayout(0, m)
+    for m in range(len(PARTS)):
         for d in (1, 3, 2):
-            sends[GX - d, s].wait_recv()
-            if s + 2 < SUB:
-                sends[GX - d, s + 2].start()
-            relayout(d, s)
-            if s == 3 and d == 1:
-                early.to_plane()
-        products(s)
-        if s == 2:
+            sends[GX - d, m].wait_recv()
+            if m + AHEAD < len(PARTS):
+                sends[GX - d, m + AHEAD].start()
+            relayout(d, m)
+        products(m)
+        if m == 2:
             early.to_core()
             early.from_core()
+            early.to_plane()
     late.to_core()
     late.from_core()
     late.to_plane()
@@ -246,7 +265,10 @@
         cols = slice(j * 256, (j + 1) * 256)
         t[:, cols] = jnp.dot(factor_t[...], xs[:, cols], preferred_element_type=jnp.float32).astype(jnp.bfloat16)
     for r0 in range(0, 128, 16):
-        block = jnp.concatenate([t[r0:r0 + 16, j * 256:(j + 1) * 256] for j in range(16)], axis=0)
+        halves = [
+            jnp.concatenate([t[r0:r0 + 16, h + j * 128:h + (j + 1) * 128] for j in range(16)], axis=0) for h in (0, 2048)
+        ]
+        block = jnp.concatenate(halves, axis=1)
         rows = jnp.dot(perm[...], block, preferred_element_type=jnp.float32).astype(jnp.bfloat16)
         buf[r0:r0 + 16] = rows.reshape(16, 16, 256)
     pl.semaphore_wait(barrier, len(near))
@@ -345,18 +367,28 @@
 
 
 def factor_kernel(packed, sketch, factor, factor_t, gram, basis, image, a, d, diagonal):
-    for s in range(SUB):
-        for r in range(s + 1):
-            block = packed[FIRST[s] + 128 * r:FIRST[s] + 128 * r + 128, :]
-            gram[128 * r:128 * r + 128, 128 * s:128 * s + 128] = block
-            if r < s:
-                gram[128 * s:128 * s + 128, 128 * r:128 * r + 128] = block.T
-    start = jnp.concatenate(
-        [sketch[128 * b + 32 * s:128 * b + 32 * s + 32, :] for s in range(SUB) for b in range(GX)], axis=0
-    ).T
     row = lax.broadcasted_iota(jnp.int32, (128, 128), 0)
     col = lax.broadcasted_iota(jnp.int32, (128, 128), 1)
 
+    def put(r, c, block):
+        gram[128 * r:128 * r + 128, 128 * c:128 * c + 128] = block
+        if r < c:
+            gram[128 * c:128 * c + 128, 128 * r:128 * r + 128] = block.T
+
+    for c in range(3):
+        for r in range(c + 1):
+            put(r, c, packed[FIRST[c] + 128 * r:FIRST[c] + 128 * r + 128, :])
+    third = packed[FIRST[3]:FIRST[3] + 224, :]
+    third = jnp.concatenate([third[:, :64], third[:, 64:], jnp.zeros((64, 64), jnp.float32)], axis=0)
+    fourth = packed[FIRST[4]:FIRST[4] + 256, :]
+    fourth = jnp.concatenate([fourth[:, :64], fourth[:, 64:]], axis=0)
+    panel = jnp.concatenate([third, fourth], axis=1)
+    for r in range(3):
+        put(r, 3, panel[128 * r:128 * r + 128, :])
+    corner = panel[384:512, :]
+    put(3, 3, jnp.where((row >= 64) & (col < 64), corner.T, corner))
+    order = [(128 * b + START[k], BASE[k] + b * LENGTH[k], LENGTH[k]) for k in range(len(LENGTH)) for b in range(GX)]
+    start = jnp.concatenate([sketch[at:at + n, :] for at, _, n in order], axis=0).T
     def orthonormalize():
         inner = exact_dot(image[...], image[...], ((1,), (1,)))
         a[...] = inner
@@ -368,9 +400,8 @@
     def finish():
         factor_t[...] = basis[...].astype(jnp.bfloat16)
         final = basis[...].T
-        for s in range(SUB):
-            for b in range(GX):
-                factor[128 * b + 32 * s:128 * b + 32 * s + 32, :] = final[128 * s + 32 * b:128 * s + 32 * b + 32, :]
+        for at, place, n in order:
+            factor[at:at + n, :] = final[place:place + n, :]
 
     first = exact_dot(start, gram[...])
     first = first * lax.rsqrt(jnp.sum(first * first, axis=1, keepdims=True))
@@ -417,7 +448,7 @@
             pltpu.VMEM((PLANE, 16, 128), jnp.float32),
             pltpu.VMEM((GZ, 24, 128), jnp.float32),
             pltpu.VMEM((GZ, 16, 128), jnp.float32),
-            DMA((GX * SUB,)), DMA((GX * SUB,)), DMA,
+            DMA((GX * len(PARTS),)), DMA((GX * len(PARTS),)), DMA,
             DMA((2,)), DMA((2,)),
             DMA((2, PLANE)), DMA((2, PLANE)),
             DMA((2, GZ)), DMA((2, GZ)),

time: 104 us -> 104 us (level)
  no operation moved by 1% of the time
where the time goes in v6:
time: 104 us
  Pallas kernels  102 us (98%)
    pallas_call x1, Pallas kernels, shards(): pl.pallas_call(gram_kernel, out_shape=(jax.ShapeDtypeStruct((512, 4096),...  78.9 us
    pallas_call x1, Pallas kernels, shards(): pl.pallas_call(core_kernel, out_shape=jax.ShapeDtypeStruct((4, 512, 256),...  16.5 us
    pallas_call x1, Pallas kernels, shards(): pl.pallas_call(factor_kernel, out_shape=(jax.ShapeDtypeStruct((512, 128),...  7 us

profile of v6, /device:TPU:1, one launch (start us, length us, event | category | flops | bytes accessed | tf_op | source)
XLA Modules:
  0.0 104.1 jit_solution(10136917429716031001)
XLA Ops:
  0.6 0.0 copy-start
  0.6 78.9 %gram.1 = (bf16[512,4096]{1,0:T(8,128)(2,1)S(1)}, f32[1280,128]{1,0:T(8,128)S(1)}) custom-call(bf16[128,64,256]{2,1,0:T(8,128)(2,1)} %field.1), custom_call_target="tpu_custom_call" | custom-call | tf_op jit(solution)/shard_map/gram/pallas_call | solution.py:433
  79.6 0.0 copy-done
  79.6 7.0 %factor.1 = (f32[512,128]{1,0:T(8,128)}, bf16[128,512]{1,0:T(8,128)(2,1)S(1)}) custom-call(f32[1280,128]{1,0:T(8,128)S(1)} %get-tuple-element.6.packed, f32[512,128]{1,0:T(8,128)S(1)} %copy-done), custom_call_target="tpu_custom_call" | custom-call | tf_op jit(solution)/shard_map/factor/pallas_call | solution.py:463
  86.6 16.5 %core.1 = bf16[4,512,256]{2,1,0:T(8,128)(2,1)S(1)} custom-call(bf16[128,512]{1,0:T(8,128)(2,1)S(1)} %get-tuple-element.8.factor_t, bf16[512,4096]{1,0:T(8,128)(2,1)S(1)} %get-tuple-element.9.xs), custom_call_target="tpu_custom_call" | custom-call | tf_op jit(solution)/shard_map/core/pallas_call | solution.py:482
  103.1 1.0 copy.5
Async XLA Ops:
  0.6 78.9 %copy-start = (f32[512,128]{1,0:T(8,128)S(1)}, f32[512,128]{1,0:T(8,128)}, u32[]{:S(2)}) copy-start(f32[512,128]{1,0:T(8,128)} %sketch.1) | copy-start | bytes 786436

commit v7 on v6

--- a/solution.py
+++ b/solution.py
@@ -18,7 +18,7 @@
 LAST = 4
 FIRST = (0, 128, 384, 768, 1024)
 PARTS = ((0, (0, 1)), (1, (0, 1)), (2, (0, 1)), (3, (0, 1)), (4, (0,)), (4, (1,)))
-AHEAD = 6
+AHEAD = 3
 
 
 def remote(src, dst, send, recv, dev):
@@ -253,8 +253,9 @@
         return min(dx, GX - dx) + min(dy, YC - dy)
 
     offsets = [(dx, dy, f) for dx in range(GX) for dy in range(YC) for f in range(2) if dx or dy or f]
-    near = sorted((o for o in offsets if hops(*o[:2]) <= 2), key=lambda o: -hops(*o[:2]))
-    far = sorted((o for o in offsets if hops(*o[:2]) > 2), key=lambda o: -hops(*o[:2]))
+    ring = [sorted((o for o in offsets if hops(*o[:2]) == n), key=lambda o: o[2]) for n in range(5)]
+    near, two, far = ring[1] + ring[0], ring[2], ring[4] + ring[3]
+    sides = [dev(1, 0, 0), dev(3, 0, 0), dev(0, 1, 0), dev(0, 3, 0)]
     corners = [dev(1, 1, 0), dev(3, 3, 0)]
     barrier = pltpu.get_barrier_semaphore()
     for o in near:
@@ -272,8 +273,8 @@
         rows = jnp.dot(perm[...], block, preferred_element_type=jnp.float32).astype(jnp.bfloat16)
         buf[r0:r0 + 16] = rows.reshape(16, 16, 256)
     pl.semaphore_wait(barrier, len(near))
-    for corner in corners:
-        pl.semaphore_signal(ready, inc=1, device_id=corner, device_id_type=MESH)
+    for side in sides:
+        pl.semaphore_signal(ready.at[0], inc=1, device_id=side, device_id_type=MESH)
 
     def place(px, py):
         return out.at[:, pl.ds(pl.multiple_of(py * 64 + px * 16, 16), 16), :]
@@ -289,17 +290,21 @@
         copies.append(remote(src, place(x, y), send.at[number(*o)], recv.at[number(*o)], dev(*o)))
         copies[-1].start()
 
-    two = [o for o in near if hops(*o[:2]) == 2]
+    for o in near:
+        push(o)
+    pl.semaphore_wait(ready.at[0], len(sides))
+    for corner in corners:
+        pl.semaphore_signal(ready.at[1], inc=1, device_id=corner, device_id_type=MESH)
     for o in two:
         push(o)
-    pl.semaphore_wait(ready, len(corners))
-    for o in far + near[len(two):]:
+    pl.semaphore_wait(ready.at[1], len(corners))
+    for o in far:
         push(o)
     mine = pltpu.make_async_copy(buf.at[pl.ds(x * 32 + y * 4, 4)], place(x, y), own_sem)
     mine.start()
     for c in copies:
         c.wait_send()
-    for dx, dy, f in near + far:
+    for dx, dy, f in near + two + far:
         at = place(*there(-dx, -dy, f))
         n = number(dx, dy, f)
         remote(at, at, send.at[n], recv.at[n], dev(dx, dy, f)).wait_recv()
@@ -489,7 +494,7 @@
             pltpu.VMEM((128, 4096), jnp.bfloat16),
             pltpu.VMEM((128, 16, 256), jnp.bfloat16),
             DMA((GX * GY,)), DMA((GX * GY,)), DMA,
-            pltpu.SemaphoreType.REGULAR,
+            pltpu.SemaphoreType.REGULAR((2,)),
         ],
         compiler_params=pltpu.CompilerParams(
             collective_id=1, has_side_effects=True, vmem_limit_bytes=20 * 2**20

time: 104 us -> 104 us (level)
    pallas_call x1, Pallas kernels: 78.9 us -> 77.9 us  [shards(): pl.pallas_call(gram_kernel, out_shape=(jax.ShapeDtypeStruct((512, 4096),...]
where the time goes in v7:
time: 104 us
  Pallas kernels  102 us (98%)
    pallas_call x1, Pallas kernels, shards(): pl.pallas_call(gram_kernel, out_shape=(jax.ShapeDtypeStruct((512, 4096),...  77.9 us
    pallas_call x1, Pallas kernels, shards(): pl.pallas_call(core_kernel, out_shape=jax.ShapeDtypeStruct((4, 512, 256),...  17 us
    pallas_call x1, Pallas kernels, shards(): pl.pallas_call(factor_kernel, out_shape=(jax.ShapeDtypeStruct((512, 128),...  7 us

profile of v7, /device:TPU:1, one launch (start us, length us, event | category | flops | bytes accessed | tf_op | source)
XLA Modules:
  0.0 103.5 jit_solution(143030322141684459)
XLA Ops:
  0.6 0.0 copy-start
  0.6 77.9 %gram.1 = (bf16[512,4096]{1,0:T(8,128)(2,1)S(1)}, f32[1280,128]{1,0:T(8,128)S(1)}) custom-call(bf16[128,64,256]{2,1,0:T(8,128)(2,1)} %field.1), custom_call_target="tpu_custom_call" | custom-call | tf_op jit(solution)/shard_map/gram/pallas_call | solution.py:438
  78.5 0.0 copy-done
  78.5 7.0 %factor.1 = (f32[512,128]{1,0:T(8,128)}, bf16[128,512]{1,0:T(8,128)(2,1)S(1)}) custom-call(f32[1280,128]{1,0:T(8,128)S(1)} %get-tuple-element.6.packed, f32[512,128]{1,0:T(8,128)S(1)} %copy-done), custom_call_target="tpu_custom_call" | custom-call | tf_op jit(solution)/shard_map/factor/pallas_call | solution.py:468
  85.5 17.0 %core.1 = bf16[4,512,256]{2,1,0:T(8,128)(2,1)S(1)} custom-call(bf16[128,512]{1,0:T(8,128)(2,1)S(1)} %get-tuple-element.8.factor_t, bf16[512,4096]{1,0:T(8,128)(2,1)S(1)} %get-tuple-element.9.xs), custom_call_target="tpu_custom_call" | custom-call | tf_op jit(solution)/shard_map/core/pallas_call | solution.py:487
  102.6 1.0 copy.5
Async XLA Ops:
  0.6 77.9 %copy-start = (f32[512,128]{1,0:T(8,128)S(1)}, f32[512,128]{1,0:T(8,128)}, u32[]{:S(2)}) copy-start(f32[512,128]{1,0:T(8,128)} %sketch.1) | copy-start | bytes 786436

commit v8 on v7

--- a/solution.py
+++ b/solution.py
@@ -19,6 +19,7 @@
 FIRST = (0, 128, 384, 768, 1024)
 PARTS = ((0, (0, 1)), (1, (0, 1)), (2, (0, 1)), (3, (0, 1)), (4, (0,)), (4, (1,)))
 AHEAD = 3
+ORDER = [(128 * b + START[k], BASE[k] + b * LENGTH[k], LENGTH[k]) for k in range(len(LENGTH)) for b in range(GX)]
 
 
 def remote(src, dst, send, recv, dev):
@@ -371,7 +372,7 @@
     return lax.dot_general(u, v, (dims, ((), ())), precision=lax.Precision.HIGHEST, preferred_element_type=jnp.float32)
 
 
-def factor_kernel(packed, sketch, factor, factor_t, gram, basis, image, a, d, diagonal):
+def factor_kernel(packed, sketch, basis, factor_t, gram, image, a, d, diagonal):
     row = lax.broadcasted_iota(jnp.int32, (128, 128), 0)
     col = lax.broadcasted_iota(jnp.int32, (128, 128), 1)
 
@@ -392,8 +393,7 @@
         put(r, 3, panel[128 * r:128 * r + 128, :])
     corner = panel[384:512, :]
     put(3, 3, jnp.where((row >= 64) & (col < 64), corner.T, corner))
-    order = [(128 * b + START[k], BASE[k] + b * LENGTH[k], LENGTH[k]) for k in range(len(LENGTH)) for b in range(GX)]
-    start = jnp.concatenate([sketch[at:at + n, :] for at, _, n in order], axis=0).T
+    start = jnp.concatenate([sketch[at:at + n, :] for at, _, n in ORDER], axis=0).T
     def orthonormalize():
         inner = exact_dot(image[...], image[...], ((1,), (1,)))
         a[...] = inner
@@ -404,9 +404,6 @@
 
     def finish():
         factor_t[...] = basis[...].astype(jnp.bfloat16)
-        final = basis[...].T
-        for at, place, n in order:
-            factor[at:at + n, :] = final[place:place + n, :]
 
     first = exact_dot(start, gram[...])
     first = first * lax.rsqrt(jnp.sum(first * first, axis=1, keepdims=True))
@@ -427,6 +424,21 @@
 
         lax.fori_loop(0, ITERS, sweep, 0)
         finish()
+
+
+def store_kernel(core, basis, out, factor, rows, sem):
+    copies = [pltpu.make_async_copy(core.at[r], out.at[r], sem.at[r]) for r in range(core.shape[0])]
+    for c in copies:
+        c.start()
+    for c in range(4):
+        final = basis[:, 128 * c:128 * c + 128].T
+        for at, place, n in ORDER:
+            if place // 128 == c:
+                rows[at:at + n, :] = final[place - 128 * c:place - 128 * c + n, :]
+    copies.append(pltpu.make_async_copy(rows, factor, sem.at[4]))
+    copies[-1].start()
+    for c in copies:
+        c.wait()
 
 
 VMEM = pl.BlockSpec(memory_space=pltpu.VMEM)
@@ -465,17 +477,16 @@
         ),
         name="gram",
     )(pltpu.with_memory_space_constraint(field, pltpu.HBM))
-    factor, factor_t = pl.pallas_call(
+    basis, factor_t = pl.pallas_call(
         factor_kernel,
         out_shape=(
-            jax.ShapeDtypeStruct((512, 128), jnp.float32),
+            jax.ShapeDtypeStruct((128, 512), jnp.float32),
             jax.ShapeDtypeStruct((128, 512), jnp.bfloat16),
         ),
         in_specs=[VMEM, VMEM],
         out_specs=(VMEM, VMEM),
         scratch_shapes=[
             pltpu.VMEM((512, 512), jnp.float32),
-            pltpu.VMEM((128, 512), jnp.float32),
             pltpu.VMEM((128, 512), jnp.float32),
             pltpu.VMEM((128, 128), jnp.float32),
             pltpu.VMEM((128, 128), jnp.float32),
@@ -501,6 +512,18 @@
         ),
         name="core",
     )(factor_t, xs)
+    core, factor = pl.pallas_call(
+        store_kernel,
+        out_shape=(
+            jax.ShapeDtypeStruct((4, 512, 256), jnp.bfloat16),
+            jax.ShapeDtypeStruct((512, 128), jnp.float32),
+        ),
+        in_specs=[VMEM, VMEM],
+        out_specs=(ANY, ANY),
+        scratch_shapes=[pltpu.VMEM((512, 128), jnp.float32), DMA((5,))],
+        compiler_params=pltpu.CompilerParams(vmem_limit_bytes=16 * 2**20),
+        name="store",
+    )(core, basis)
     return (factor, core)
 
 

time: 104 us -> 103 us (level)
    pallas_call x1 -> x2, Pallas kernels: 7 us -> 7.27 us  [the longest x1 6.18 us: shards(): pl.pallas_call(factor_kernel, out_shape=(jax.ShapeDtypeStruct((128, 512),...]
where the time goes in v8:
time: 103 us
  Pallas kernels  102 us (99%)
    pallas_call x1, Pallas kernels, shards(): pl.pallas_call(gram_kernel, out_shape=(jax.ShapeDtypeStruct((512, 4096),...  77.9 us
    pallas_call x1, Pallas kernels, shards(): pl.pallas_call(core_kernel, out_shape=jax.ShapeDtypeStruct((4, 512, 256),...  17.2 us
    pallas_call x1, Pallas kernels, shards(): pl.pallas_call(factor_kernel, out_shape=(jax.ShapeDtypeStruct((128, 512),...  6.18 us

profile of v8, /device:TPU:1, one launch (start us, length us, event | category | flops | bytes accessed | tf_op | source)
XLA Modules:
  0.0 103.2 jit_solution(9538944247888806847)
XLA Ops:
  0.6 0.0 copy-start
  0.6 77.9 %gram.1 = (bf16[512,4096]{1,0:T(8,128)(2,1)S(1)}, f32[1280,128]{1,0:T(8,128)S(1)}) custom-call(bf16[128,64,256]{2,1,0:T(8,128)(2,1)} %field.1), custom_call_target="tpu_custom_call" | custom-call | tf_op jit(solution)/shard_map/gram/pallas_call | solution.py:450
  78.5 0.0 copy-done
  78.5 6.2 %factor.1 = (f32[128,512]{1,0:T(8,128)S(1)}, bf16[128,512]{1,0:T(8,128)(2,1)S(1)}) custom-call(f32[1280,128]{1,0:T(8,128)S(1)} %get-tuple-element.8.packed, f32[512,128]{1,0:T(8,128)S(1)} %copy-done), custom_call_target="tpu_custom_call" | custom-call | tf_op jit(solution)/shard_map/factor/pallas_call | solution.py:480
  84.7 17.2 %core.1 = bf16[4,512,256]{2,1,0:T(8,128)(2,1)S(1)} custom-call(bf16[128,512]{1,0:T(8,128)(2,1)S(1)} %get-tuple-element.9.factor_t, bf16[512,4096]{1,0:T(8,128)(2,1)S(1)} %get-tuple-element.10.xs), custom_call_target="tpu_custom_call" | custom-call | tf_op jit(solution)/shard_map/core/pallas_call | solution.py:498
  101.9 1.1 %store.1 = (bf16[4,512,256]{2,1,0:T(8,128)(2,1)}, f32[512,128]{1,0:T(8,128)}) custom-call(bf16[4,512,256]{2,1,0:T(8,128)(2,1)S(1)} %core.1, f32[128,512]{1,0:T(8,128)S(1)} %get-tuple-element.11.basis), custom_call_target="tpu_custom_call" | custom-call | tf_op jit(solution)/shard_map/store/pallas_call | solution.py:515
Async XLA Ops:
  0.6 77.9 %copy-start = (f32[512,128]{1,0:T(8,128)S(1)}, f32[512,128]{1,0:T(8,128)}, u32[]{:S(2)}) copy-start(f32[512,128]{1,0:T(8,128)} %sketch.1) | copy-start | bytes 786436

commit v9 on v8

--- a/solution.py
+++ b/solution.py
@@ -226,13 +226,12 @@
     late.to_line()
     early.from_line()
     early.spread()
-    for c in sends.values():
-        c.wait_send()
-    settle()
     late.from_line()
     late.spread()
     early.gather()
     early.finish()
+    for c in sends.values():
+        c.wait_send()
     settle()
     late.gather()
     settle()

time: 103 us -> 103 us (level)
  no operation moved by 1% of the time
where the time goes in v9:
time: 103 us
  Pallas kernels  102 us (99%)
    pallas_call x1, Pallas kernels, shards(): pl.pallas_call(gram_kernel, out_shape=(jax.ShapeDtypeStruct((512, 4096),...  77.9 us
    pallas_call x1, Pallas kernels, shards(): pl.pallas_call(core_kernel, out_shape=jax.ShapeDtypeStruct((4, 512, 256),...  17.2 us
    pallas_call x1, Pallas kernels, shards(): pl.pallas_call(factor_kernel, out_shape=(jax.ShapeDtypeStruct((128, 512),...  6.18 us

profile of v9, /device:TPU:1, one launch (start us, length us, event | category | flops | bytes accessed | tf_op | source)
XLA Modules:
  0.0 103.2 jit_solution(13448579334262549871)
XLA Ops:
  0.6 0.0 copy-start
  0.6 77.9 %gram.1 = (bf16[512,4096]{1,0:T(8,128)(2,1)S(1)}, f32[1280,128]{1,0:T(8,128)S(1)}) custom-call(bf16[128,64,256]{2,1,0:T(8,128)(2,1)} %field.1), custom_call_target="tpu_custom_call" | custom-call | tf_op jit(solution)/shard_map/gram/pallas_call | solution.py:449
  78.5 0.0 copy-done
  78.5 6.2 %factor.1 = (f32[128,512]{1,0:T(8,128)S(1)}, bf16[128,512]{1,0:T(8,128)(2,1)S(1)}) custom-call(f32[1280,128]{1,0:T(8,128)S(1)} %get-tuple-element.8.packed, f32[512,128]{1,0:T(8,128)S(1)} %copy-done), custom_call_target="tpu_custom_call" | custom-call | tf_op jit(solution)/shard_map/factor/pallas_call | solution.py:479
  84.7 17.2 %core.1 = bf16[4,512,256]{2,1,0:T(8,128)(2,1)S(1)} custom-call(bf16[128,512]{1,0:T(8,128)(2,1)S(1)} %get-tuple-element.9.factor_t, bf16[512,4096]{1,0:T(8,128)(2,1)S(1)} %get-tuple-element.10.xs), custom_call_target="tpu_custom_call" | custom-call | tf_op jit(solution)/shard_map/core/pallas_call | solution.py:497
  101.9 1.1 %store.1 = (bf16[4,512,256]{2,1,0:T(8,128)(2,1)}, f32[512,128]{1,0:T(8,128)}) custom-call(bf16[4,512,256]{2,1,0:T(8,128)(2,1)S(1)} %core.1, f32[128,512]{1,0:T(8,128)S(1)} %get-tuple-element.11.basis), custom_call_target="tpu_custom_call" | custom-call | tf_op jit(solution)/shard_map/store/pallas_call | solution.py:514
Async XLA Ops:
  0.6 77.9 %copy-start = (f32[512,128]{1,0:T(8,128)S(1)}, f32[512,128]{1,0:T(8,128)}, u32[]{:S(2)}) copy-start(f32[512,128]{1,0:T(8,128)} %sketch.1) | copy-start | bytes 786436
